TPU v7x, 128 devices: a whole 4x4x4 slice. The times are simulated.
128 devices in a mesh: dp: 16 (over x, z), row: 4 (over y_lo, core), col: 2 (over y_hi).
Axes of the slice: x: 4, y: 4 (y_hi: 2, y_lo: 2; y = y_hi * 2 + y_lo), z: 4, core: 2. Of those that a mesh axis runs over, the one named last changes fastest.
Arguments:
- tokens: bfloat16 [16, 1024, 1536], P('dp', 'col', 'row'), may hold values from -6 to 6
- gain1: float32 [1536], P('row'), may hold values from 0.1 to 1.9
- w_query: bfloat16 [1536, 1536], P('row', 'col'), may hold values from -0.15625 to 0.15625
- w_keyval: bfloat16 [1536, 1536], P('row', 'col'), may hold values from -0.15625 to 0.15625
- w_out: bfloat16 [1536, 1536], P('col', 'row'), may hold values from -0.4375 to 0.4375
- gain2: float32 [1536], P('row'), may hold values from 0.1 to 1.9
- w_gate: bfloat16 [1536, 4096], P('row', 'col'), may hold values from -0.15625 to 0.15625
- w_up: bfloat16 [1536, 4096], P('row', 'col'), may hold values from -0.15625 to 0.15625
- w_down: bfloat16 [4096, 1536], P('col', 'row'), may hold values from -0.09375 to 0.09375
- grad_out: bfloat16 [16, 1024, 1536], P('dp', 'col', 'row'), may hold values from -6 to 6
- segments: int32 [16, 1024], P('dp'), may hold values from 0 to 3, as said below
Outputs:
- output: bfloat16 [16, 1024, 1536], P('dp', 'col', 'row')
- grad_in: float32 [16, 1024, 1536], P('dp', 'col', 'row')
- grad_gain1: float32 [1536], P('row')
- grad_w_query: float32 [1536, 1536], P('row', 'col')
- grad_w_keyval: float32 [1536, 1536], P('row', 'col')
- grad_w_out: float32 [1536, 1536], P('col', 'row')
- grad_gain2: float32 [1536], P('row')
- gate_weight_gradient: float32 [1536, 4096], P('row', 'col')
- up_weight_gradient: float32 [1536, 4096], P('row', 'col')
- grad_w_down: float32 [4096, 1536], P('col', 'row')
Inputs may be any that keep to these rules, and one draw needn't show every extreme that they name: `segments`: in each sequence the numbers start at 0, never fall and rise by one at each document start; each sequence holds 4 documents, which start at multiples of 64 and never at 512.
All inputs are finite; a program needn't handle non-finite values.
Results may differ from a plain program's by a relative error of at most 0.025.
Values may be sent and summed in bfloat16 or wider, within the bound.
No kernel may reach another device: no remote copies, remote signals or barrier semaphores. Data moves between devices by JAX's collectives and lax.ppermute only.
A program may use at most 128 MiB of HBM per device.

v0:
```python
import jax
import jax.numpy as jnp
from jax import lax
from jax.sharding import PartitionSpec as P

D = 1536
HD = 96
QBLK = 512
GQ = 2


EPS = 1e-05
THETA = 100000.0
NEGATIVE = -1e30


def from_everyone(value, axis):
    copies = jnp.broadcast_to(value, (lax.axis_size(axis), *value.shape))
    return lax.all_to_all(copies, axis, split_axis=0, concat_axis=0, tiled=True)


def over_copies(value, axis):
    return from_everyone(value, axis).sum(axis=0)


def laid_out(blocks, dim):
    lengths = list(blocks.shape[1:])
    lengths[dim] *= blocks.shape[0]
    return jnp.moveaxis(blocks, 0, dim).reshape(lengths)


def collect(value, axis, dim):
    blocks = from_everyone(value, axis)
    return laid_out(blocks, dim)


def cut_along(value, dim, count):
    lengths = value.shape
    blocks = value.reshape(*lengths[:dim], count, lengths[dim] // count, *lengths[dim + 1 :])
    return jnp.moveaxis(blocks, dim, 0)


def summed_on_arrival(value, axis, dim):
    count = lax.axis_size(axis)
    blocks = lax.all_to_all(cut_along(value, dim, count), axis, 0, 0, tiled=True)
    return jnp.sum(blocks.astype(jnp.float32), axis=0)


def gather_turned(arrays, axis, dims):
    turned = [jnp.moveaxis(a, dim, 0) for a, dim in zip(arrays, dims)]
    widths = [t[0].size for t in turned]
    both = jnp.concatenate([t.reshape(-1, w) for t, w in zip(turned, widths)], axis=1)
    result = lax.all_gather(both, axis, axis=0, tiled=True)
    blocks = jnp.split(result, [sum(widths[:k]) for k in range(1, len(widths))], axis=1)
    return tuple(
        (
            jnp.moveaxis(b.reshape(-1, *t.shape[1:]), 0, dim)
            for b, t, dim in zip(blocks, turned, dims)
        )
    )


def together(arrays, axis):
    vector, at, gathered = (jnp.concatenate([a.reshape(-1) for a in arrays]), 0, [])
    total = over_copies(vector, axis)
    for a in arrays:
        gathered.append(total[at : at + a.size].reshape(a.shape))
        at += a.size
    return tuple(gathered)


def rope_tables(segments):
    length = segments.shape[1]
    places = jnp.arange(length, dtype=jnp.int32)[None, :]
    starts = jnp.concatenate(
        [jnp.ones((segments.shape[0], 1), dtype=bool), segments[:, 1:] != segments[:, :-1]], axis=1
    )
    leading_factor = lax.cummax(jnp.where(starts, places, 0), axis=1)
    rates = THETA ** (-jnp.arange(HD // 2, dtype=jnp.float32) * 2.0 / HD)
    angles = (places - leading_factor).astype(jnp.float32)[..., None] * rates
    return (jnp.cos(angles), jnp.sin(angles))


def rotate(values, cosine, sine, sign):
    halfway = values.shape[-1] // 2
    front = values[..., :halfway]
    behind = values[..., halfway:]
    return jnp.concatenate(
        [front * cosine - sign * behind * sine, behind * cosine + sign * front * sine], axis=-1
    )


def norm_inverse(values):
    squares = over_copies(jnp.sum(values * values, axis=-1), "row")
    return lax.rsqrt(squares / D + EPS)[..., None]


def norm_back(grad_normed, normed, inverse, gain):
    grad_scaled = grad_normed * gain
    inner = over_copies(jnp.sum(grad_scaled * normed, axis=-1), "row")
    grad_values = inverse * (grad_scaled - normed * (inner / D)[..., None])
    gain_part = jnp.sum(grad_normed * normed, axis=(0, 1))
    return (grad_values, gain_part)


def project_in(normed, leading_factor, trailing_factor):
    collected_blocks = collect(normed, "col", 1)
    assembled_weight = lax.all_gather(collected_blocks, "row", axis=2, tiled=True)
    columns = (
        lax.all_to_all(leading_factor, "row", split_axis=1, concat_axis=0, tiled=True),
        lax.all_to_all(trailing_factor, "row", split_axis=1, concat_axis=0, tiled=True),
    )
    sums = (
        jnp.einsum("tjp,pq->tjq", assembled_weight, columns[0], preferred_element_type=jnp.float32),
        jnp.einsum("tjp,pq->tjq", assembled_weight, columns[1], preferred_element_type=jnp.float32),
    )
    return (collected_blocks, sums[0], sums[1])


def project_out(values, weight_matrix):
    collected_blocks = lax.all_gather(values, "row", axis=2, tiled=True)
    partial_summand = jnp.einsum(
        "acx,xz->acz", collected_blocks, weight_matrix, preferred_element_type=jnp.float32
    )
    return (collected_blocks, summed_on_arrival(partial_summand.astype(jnp.bfloat16), "col", 1))


def back_out(grad, weight_matrix):
    collected_blocks = collect(grad, "col", 1)
    assembled_weight = lax.all_gather(collected_blocks, "row", axis=2, tiled=True)
    columns = lax.all_to_all(weight_matrix, "row", split_axis=0, concat_axis=1, tiled=True)
    summed = jnp.einsum(
        "fkr,nr->fkn", assembled_weight, columns, preferred_element_type=jnp.float32
    )
    return (collected_blocks, summed)


def back_in(leading_factor, trailing_factor, leading_weight, trailing_weight):
    assembled_weight = gather_turned((leading_factor, trailing_factor), "row", (2, 2))
    partial_summand = jnp.einsum(
        "rzk,yk->rzy", assembled_weight[0], leading_weight, preferred_element_type=jnp.float32
    )
    partial_summand = partial_summand + jnp.einsum(
        "rzk,yk->rzy", assembled_weight[1], trailing_weight, preferred_element_type=jnp.float32
    )
    return (
        assembled_weight[0],
        assembled_weight[1],
        summed_on_arrival(partial_summand.astype(jnp.bfloat16), "col", 1),
    )


def masked_scores(query_block, keys, segment_block, row_block, segment_ids):
    columns = jnp.arange(segment_ids.shape[0], dtype=jnp.int32)
    logits = jnp.einsum(
        "qkgd,tkd->kgqt", query_block, keys, preferred_element_type=jnp.float32
    ) * HD ** (-0.5)
    allowed = (segment_block[:, None] == segment_ids[None, :]) & (
        columns[None, :] <= row_block[:, None]
    )
    return jnp.where(allowed, logits, NEGATIVE)


def attend_forward(inputs):
    queries, keys, values, segment_ids = inputs
    length, groups = (keys.shape[0], keys.shape[1])
    blocks = length // QBLK

    def one_block(pieces):
        query_block, start = pieces
        segment_block = lax.dynamic_slice_in_dim(segment_ids, start, QBLK)
        row_block = start + jnp.arange(QBLK, dtype=jnp.int32)
        logits = masked_scores(query_block, keys, segment_block, row_block, segment_ids)
        peak = jnp.max(logits, axis=-1, keepdims=True)
        weights = jnp.exp(logits - peak)
        total = jnp.sum(weights, axis=-1, keepdims=True)
        probs = (weights / total).astype(jnp.bfloat16)
        attended = jnp.einsum("kgqt,tkd->qkgd", probs, values, preferred_element_type=jnp.float32)
        return (attended.astype(jnp.bfloat16), (peak + jnp.log(total))[..., 0])

    starts = jnp.arange(blocks, dtype=jnp.int32) * QBLK
    attended, lse_all = lax.map(one_block, (queries.reshape(blocks, QBLK, groups, GQ, HD), starts))
    return (attended.reshape(length, groups, GQ, HD), lse_all)


def attend_backward(inputs):
    queries, keys, values, segment_ids, grads, lse_all = inputs
    length, groups = (keys.shape[0], keys.shape[1])
    blocks = length // QBLK
    scale = HD ** (-0.5)

    def one_block(carry, pieces):
        key_total, value_total = carry
        query_block, grad_block, lse_block, start = pieces
        segment_block = lax.dynamic_slice_in_dim(segment_ids, start, QBLK)
        row_block = start + jnp.arange(QBLK, dtype=jnp.int32)
        logits = masked_scores(query_block, keys, segment_block, row_block, segment_ids)
        probs = jnp.exp(logits - lse_block[..., None])
        grad_probs = jnp.einsum(
            "qkgd,tkd->kgqt", grad_block, values, preferred_element_type=jnp.float32
        )
        inner = jnp.sum(probs * grad_probs, axis=-1, keepdims=True)
        grad_logits = (probs * (grad_probs - inner)).astype(jnp.bfloat16)
        grad_query = (
            jnp.einsum("kgqt,tkd->qkgd", grad_logits, keys, preferred_element_type=jnp.float32)
            * scale
        )
        key_total = (
            key_total
            + jnp.einsum(
                "kgqt,qkgd->tkd", grad_logits, query_block, preferred_element_type=jnp.float32
            )
            * scale
        )
        value_total = value_total + jnp.einsum(
            "kgqt,qkgd->tkd",
            probs.astype(jnp.bfloat16),
            grad_block,
            preferred_element_type=jnp.float32,
        )
        return ((key_total, value_total), grad_query)

    starts = jnp.arange(blocks, dtype=jnp.int32) * QBLK
    empty = jnp.zeros((length, groups, HD), jnp.float32)
    (key_total, value_total), grad_queries = lax.scan(
        one_block,
        (empty, empty),
        (
            queries.reshape(blocks, QBLK, groups, GQ, HD),
            grads.reshape(blocks, QBLK, groups, GQ, HD),
            lse_all,
            starts,
        ),
    )
    return (grad_queries.reshape(length, groups, GQ, HD), key_total, value_total)


def body(tokens, gain1, w_query, w_keyval, w_out, gain2, w_gate, w_up, w_down, grad_out, segments):
    inputs_f = tokens.astype(jnp.float32)
    seqs, length = segments.shape
    cosine, sine = rope_tables(segments)
    inverse_one = norm_inverse(inputs_f)
    normed_one = inputs_f * inverse_one
    first_row_group, query_raw, keyval_raw = project_in(
        (normed_one * gain1).astype(jnp.bfloat16), w_query, w_keyval
    )
    groups = keyval_raw.shape[2] // (2 * HD)
    query_raw = query_raw.reshape(seqs, length, groups, GQ, HD)
    keyval_raw = keyval_raw.reshape(seqs, length, groups, 2, HD)
    cos_heads = cosine[:, :, None, None]
    sin_heads = sine[:, :, None, None]
    cos_keys = cosine[:, :, None]
    sin_keys = sine[:, :, None]
    query_low = rotate(query_raw, cos_heads, sin_heads, 1.0).astype(jnp.bfloat16)
    key_low = rotate(keyval_raw[:, :, :, 0], cos_keys, sin_keys, 1.0).astype(jnp.bfloat16)
    value_low = keyval_raw[:, :, :, 1].astype(jnp.bfloat16)
    attended, lse_all = lax.map(attend_forward, (query_low, key_low, value_low, segments))
    head_rows_flat, attn_part = project_out(attended.reshape(seqs, length, groups * GQ * HD), w_out)
    mixed = inputs_f + attn_part
    inverse_two = norm_inverse(mixed)
    normed_two = mixed * inverse_two
    second_row_group, gate, upward = project_in(
        (normed_two * gain2).astype(jnp.bfloat16), w_gate, w_up
    )
    hidden = (jax.nn.silu(gate) * upward).astype(jnp.bfloat16)
    hidden_state_rows, mlp_part = project_out(hidden, w_down)
    output = (mixed + mlp_part).astype(jnp.bfloat16)
    grad_top = grad_out.astype(jnp.float32)
    feedforward_gradient_rows, grad_hidden = back_out(grad_out, w_down)
    grad_w_down = jnp.einsum(
        "prc,pry->cy",
        hidden_state_rows,
        feedforward_gradient_rows,
        preferred_element_type=jnp.float32,
    )
    sigma_gate = jax.nn.sigmoid(gate)
    grad_gate = (grad_hidden * upward * sigma_gate * (1.0 + gate * (1.0 - sigma_gate))).astype(
        jnp.bfloat16
    )
    grad_upward = (grad_hidden * gate * sigma_gate).astype(jnp.bfloat16)
    full_gate_weight, full_up_weight, grad_normed_two = back_in(
        grad_gate, grad_upward, w_gate, w_up
    )
    gate_weight_gradient = jnp.einsum(
        "hxo,hxu->ou", second_row_group, full_gate_weight, preferred_element_type=jnp.float32
    )
    up_weight_gradient = jnp.einsum(
        "hxo,hxu->ou", second_row_group, full_up_weight, preferred_element_type=jnp.float32
    )
    grad_mixed_norm, gain_two_part = norm_back(grad_normed_two, normed_two, inverse_two, gain2)
    grad_mixed = grad_top + grad_mixed_norm
    attention_gradient_rows, grad_heads = back_out(grad_mixed.astype(jnp.bfloat16), w_out)
    grad_w_out = jnp.einsum(
        "prc,pry->cy", head_rows_flat, attention_gradient_rows, preferred_element_type=jnp.float32
    )
    grad_heads = grad_heads.reshape(seqs, length, groups, GQ, HD).astype(jnp.bfloat16)
    grad_query, grad_key, grad_value = lax.map(
        attend_backward, (query_low, key_low, value_low, segments, grad_heads, lse_all)
    )
    grad_query = rotate(grad_query, cos_heads, sin_heads, -1.0)
    grad_key = rotate(grad_key, cos_keys, sin_keys, -1.0)
    query_grad_low = grad_query.reshape(seqs, length, groups * GQ * HD).astype(jnp.bfloat16)
    keyval_grad_low = (
        jnp.stack([grad_key, grad_value], axis=3)
        .reshape(seqs, length, groups * 2 * HD)
        .astype(jnp.bfloat16)
    )
    full_query_weight, full_key_value_weight, grad_normed_one = back_in(
        query_grad_low, keyval_grad_low, w_query, w_keyval
    )
    grad_w_query = jnp.einsum(
        "hxo,hxu->ou", first_row_group, full_query_weight, preferred_element_type=jnp.float32
    )
    grad_w_keyval = jnp.einsum(
        "hxo,hxu->ou", first_row_group, full_key_value_weight, preferred_element_type=jnp.float32
    )
    grad_inputs_norm, gain_one_part = norm_back(grad_normed_one, normed_one, inverse_one, gain1)
    grad_in = grad_mixed + grad_inputs_norm
    gain_totals = together((gain_one_part, gain_two_part), "col")
    totals = (
        lax.psum(gain_totals[0].astype(jnp.bfloat16), "dp").astype(jnp.float32),
        lax.psum(grad_w_query.astype(jnp.bfloat16), "dp").astype(jnp.float32),
        lax.psum(grad_w_keyval.astype(jnp.bfloat16), "dp").astype(jnp.float32),
        lax.psum(grad_w_out.astype(jnp.bfloat16), "dp").astype(jnp.float32),
        lax.psum(gain_totals[1].astype(jnp.bfloat16), "dp").astype(jnp.float32),
        lax.psum(gate_weight_gradient.astype(jnp.bfloat16), "dp").astype(jnp.float32),
        lax.psum(up_weight_gradient.astype(jnp.bfloat16), "dp").astype(jnp.float32),
        lax.psum(grad_w_down.astype(jnp.bfloat16), "dp").astype(jnp.float32),
    )
    return (
        output,
        grad_in,
        totals[0],
        totals[1],
        totals[2],
        totals[3],
        totals[4],
        totals[5],
        totals[6],
        totals[7],
    )


def solution(mesh):
    return jax.shard_map(
        body,
        mesh=mesh,
        in_specs=(
            P("dp", "col", "row"),
            P("row"),
            P("row", "col"),
            P("row", "col"),
            P("col", "row"),
            P("row"),
            P("row", "col"),
            P("row", "col"),
            P("col", "row"),
            P("dp", "col", "row"),
            P("dp", None),
        ),
        out_specs=(
            P("dp", "col", "row"),
            P("dp", "col", "row"),
            P("row"),
            P("row", "col"),
            P("row", "col"),
            P("col", "row"),
            P("row"),
            P("row", "col"),
            P("row", "col"),
            P("col", "row"),
        ),
        check_vma=False,
    )
```

profile of v0, /device:TPU:0, one launch (start us, length us, event | category | flops | bytes accessed | tf_op | source)
XLA Modules:
  0.0 699.1 jit_solution(7822698275144082936)
XLA Ops:
  16.3 16.5 %all_to_all.178 = bf16[2,1,512,384]{3,2,1,0:T(8,128)(2,1)} all-to-all(bf16[2,1,512,384]{3,2,1,0:T(8,128)(2,1)S(1)} %broadcast_in_dim.104), channel_id=1, replica_groups=mesh['dp'=16,'row'=4,'col'=2] {'col'}, dimensions={0} | all-to-all | bytes 1572864 | tf_op jit(solution)/shard_map/all_to_all | solution.py:19
  39.9 8.7 %all-to-all-done.2 = bf16[384,4,192]{0,2,1:T(8,128)(2,1)S(1)} async-done(((bf16[384,4,192]{0,2,1:T(8,128)(2,1)}), bf16[384,4,192]{0,2,1:T(8,128)(2,1)S(1)}, u32[]{:S(2)}, u32[]{:S(2)}) %all-to-all-start.2) | async-done | bytes 589856 | tf_op jit(solution)/shard_map/all_to_all | solution.py:110
  53.7 14.5 %all-to-all-done.3 = bf16[384,4,192]{0,2,1:T(8,128)(2,1)S(1)} async-done(((bf16[384,4,192]{0,2,1:T(8,128)(2,1)}), bf16[384,4,192]{0,2,1:T(8,128)(2,1)S(1)}, u32[]{:S(2)}, u32[]{:S(2)}) %all-to-all-start.3) | async-done | bytes 589856 | tf_op jit(solution)/shard_map/all_to_all | solution.py:111
  68.3 10.3 %all-gather.10.cloned.1.call-done = bf16[1,1024,1536]{2,1,0:T(8,128)(2,1)} async-done(((bf16[1,1024,384]{2,1,0:T(8,128)(2,1)}), bf16[1,1024,1536]{2,1,0:T(8,128)(2,1)}) %all-gather.10.cloned.1.call-update) | async-done | bytes 3145744 | tf_op jit(solution)/shard_map/all_gather | solution.py:108
  85.5 15.4 %while.47 = (s32[]{:T(128)}, bf16[2,512,1,2,96]{1,4,3,2,0:T(8,128)(2,1)S(1)}, f32[2,1,2,512]{3,2,1,0:T(2,128)S(1)}, s32[2]{0:T(128)S(1)}, s32[1024]{0:T(1024)S(1...) while((s32[]{:T(128)}, ...), condition=%wide.region_7.8_spmd, body=%wide.region_4.7_spmd.sunk | while | flops 416906752 | bytes 15513783 | solution.py:182
  102.5 19.1 %all_to_all.179 = bf16[2,1,512,384]{3,2,1,0:T(8,128)(2,1)} all-to-all(bf16[2,1,512,384]{3,2,1,0:T(8,128)(2,1)S(1)} %broadcast_in_dim.108), channel_id=1, replica_groups=mesh['dp'=16,'row'=4,'col'=2] {'col'}, dimensions={0} | all-to-all | bytes 1572864 | tf_op jit(solution)/shard_map/all_to_all | solution.py:19
  130.8 19.8 %all_to_all.180 = bf16[2,1,512,384]{3,2,1,0:T(8,128)(2,1)S(1)} all-to-all(bf16[2,1,512,384]{3,2,1,0:T(8,128)(2,1)S(1)} %bitcast.498), channel_id=1, replica_groups=mesh['dp'=16,'row'=4,'col'=2] {'col'}, dimensions={0} | all-to-all | bytes 1572864 | tf_op jit(solution)/shard_map/all_to_all | solution.py:45
  157.4 25.0 %all_to_all.182 = bf16[2,1,512,384]{3,2,1,0:T(8,128)(2,1)} all-to-all(bf16[2,1,512,384]{3,2,1,0:T(8,128)(2,1)S(1)} %broadcast_in_dim.107), channel_id=1, replica_groups=mesh['dp'=16,'row'=4,'col'=2] {'col'}, dimensions={0} | all-to-all | bytes 1572864 | tf_op jit(solution)/shard_map/all_to_all | solution.py:19
  188.5 27.0 %all-to-all-done.11 = bf16[4,512,384]{2,1,0:T(8,128)(2,1)S(1)} async-done(((bf16[4,512,384]{2,1,0:T(8,128)(2,1)}), bf16[4,512,384]{2,1,0:T(8,128)(2,1)S(1)}, u32[]{:S(2)}, u32[]{:S(2)}) %all-to-all-start.11) | async-done | bytes 1572896 | tf_op jit(solution)/shard_map/all_to_all | solution.py:131
  222.7 25.5 %all-to-all-done.7 = bf16[384,4,512]{0,2,1:T(8,128)(2,1)} async-done(((bf16[384,4,512]{0,2,1:T(8,128)(2,1)}), bf16[384,4,512]{0,2,1:T(8,128)(2,1)}, u32[]{:S(2)}, u32[]{:S(2)}) %all-to-all-start.7) | async-done | bytes 1572896 | tf_op jit(solution)/shard_map/all_to_all | solution.py:110
  256.0 16.7 %all-to-all-done.8 = bf16[384,4,512]{0,2,1:T(8,128)(2,1)} async-done(((bf16[384,4,512]{0,2,1:T(8,128)(2,1)}), bf16[384,4,512]{0,2,1:T(8,128)(2,1)}, u32[]{:S(2)}, u32[]{:S(2)}) %all-to-all-start.8) | async-done | bytes 1572896 | tf_op jit(solution)/shard_map/all_to_all | solution.py:111
  290.3 80.3 %all-gather.18.cloned.1.call-done = bf16[2048,2048]{0,1:T(8,128)(2,1)} async-done(((bf16[512,2048]{0,1:T(8,128)(2,1)}), bf16[2048,2048]{0,1:T(8,128)(2,1)}) %all-gather.18.cloned.1.call-update) | async-done | bytes 8388624 | tf_op jit(solution)/shard_map/all_gather | solution.py:53
  378.1 17.4 %all_to_all.183 = bf16[2,1,512,384]{3,2,1,0:T(8,128)(2,1)S(1)} all-to-all(bf16[2,1,512,384]{3,2,1,0:T(8,128)(2,1)S(1)} %bitcast.497), channel_id=1, replica_groups=mesh['dp'=16,'row'=4,'col'=2] {'col'}, dimensions={0} | all-to-all | bytes 1572864 | tf_op jit(solution)/shard_map/all_to_all | solution.py:45
  403.0 15.7 %all_to_all.185 = bf16[2,1,512,384]{3,2,1,0:T(8,128)(2,1)} all-to-all(bf16[2,1,512,384]{3,2,1,0:T(8,128)(2,1)S(1)} %broadcast_in_dim.110), channel_id=1, replica_groups=mesh['dp'=16,'row'=4,'col'=2] {'col'}, dimensions={0} | all-to-all | bytes 1572864 | tf_op jit(solution)/shard_map/all_to_all | solution.py:19
  422.9 11.8 %all-to-all-done.15 = bf16[4,192,384]{2,1,0:T(8,128)(2,1)} async-done(((bf16[4,192,384]{2,1,0:T(8,128)(2,1)}), bf16[4,192,384]{2,1,0:T(8,128)(2,1)}, u32[]{:S(2)}, u32[]{:S(2)}) %all-to-all-start.15) | async-done | bytes 589856 | tf_op jit(solution)/shard_map/all_to_all | solution.py:131
  439.8 18.0 %all-gather.20.cloned.1.call-done = bf16[1,1024,1536]{2,1,0:T(8,128)(2,1)} async-done(((bf16[1,1024,384]{2,1,0:T(8,128)(2,1)}), bf16[1,1024,1536]{2,1,0:T(8,128)(2,1)}) %all-gather.20.cloned.1.call-update) | async-done | bytes 3145744 | tf_op jit(solution)/shard_map/all_gather | solution.py:130
  463.8 44.2 %while.48 = (s32[]{:T(128)}, f32[1024,1,96]{0,2,1:T(8,128)S(1)}, f32[1024,1,96]{0,2,1:T(8,128)}, f32[2,512,1,2,96]{1,0,4,3,2:T(2,128)}, bf16[2,512,1,2,96]{1,4,3...) while((s32[]{:T(128)}, f32[1024,1,96]{0,2,1:T(8,128)S(1)}, ...), condition=%wide.region_17.18_spmd.clone, body=%wide.region_15.17_spmd.clone.sunk | while | flops 1024523776 | bytes 38512868 | solution.py:225
  477.8 8.1 %dynamic_update_slice.34 = f32[2,512,1,2,96]{1,0,4,3,2:T(2,128)} dynamic-update-slice(f32[2,512,1,2,96]{1,0,4,3,2:T(2,128)} %get-tuple-element.518, f32[1,512,1,2,96]{1,0,4,3,2:T(1,128)S(1)} %copy.140, s32[]{:T(128)S(6)} %copy.158, s32[]{:T(128)} %constant.90.clone.1..sunk.1, s32[]{:T(128)} %constant.90.clone.1..sunk.1, s32[]{:T(128)} %constant.90.clone.1..sunk.1, s32[]{:T(128)} %constant.90.clone.1..sunk.1) | dynamic-update-slice | bytes 786436 | tf_op jit(solution)/shard_map/while/body/eval_jaxpr/while/body/jit(dynamic_update_index_in_dim)/dynamic_update_slice | solution.py:225
  500.0 8.1 %dynamic_update_slice.34 = f32[2,512,1,2,96]{1,0,4,3,2:T(2,128)} dynamic-update-slice(f32[2,512,1,2,96]{1,0,4,3,2:T(2,128)} %get-tuple-element.518, f32[1,512,1,2,96]{1,0,4,3,2:T(1,128)S(1)} %copy.140, s32[]{:T(128)S(6)} %copy.158, s32[]{:T(128)} %constant.90.clone.1..sunk.1, s32[]{:T(128)} %constant.90.clone.1..sunk.1, s32[]{:T(128)} %constant.90.clone.1..sunk.1, s32[]{:T(128)} %constant.90.clone.1..sunk.1) | dynamic-update-slice | bytes 786436 | tf_op jit(solution)/shard_map/while/body/eval_jaxpr/while/body/jit(dynamic_update_index_in_dim)/dynamic_update_slice | solution.py:225
  532.3 17.9 %all-gather.22.cloned.1.call-done = bf16[768,2048]{1,0:T(8,128)(2,1)} async-done(((bf16[192,2048]{1,0:T(8,128)(2,1)}), bf16[768,2048]{1,0:T(8,128)(2,1)}) %all-gather.22.cloned.1.call-update) | async-done | bytes 3145744 | tf_op jit(solution)/shard_map/all_gather | solution.py:53
  564.6 6.9 convolution_convert_fusion.1
  584.8 10.5 %all-to-all-done.9 = bf16[2,1,512,384]{3,2,1,0:T(8,128)(2,1)} async-done(((bf16[2,1,512,384]{3,2,1,0:T(8,128)(2,1)}), bf16[2,1,512,384]{3,2,1,0:T(8,128)(2,1)}, u32[]{:S(2)}, u32[]{:S(2)}) %all-to-all-start.9) | async-done | bytes 786464 | tf_op jit(solution)/shard_map/all_to_all | solution.py:45
  608.3 40.6 %all-reduce = (bf16[384]{0:T(512)(128)(2,1)S(1)}, bf16[384]{0:T(512)(128)(2,1)S(1)}) all-reduce(bf16[384]{0:T(512)(128)(2,1)S(1)} %get-tuple-element.343, bf16[384]{0:T(512)(128)(2,1)S(1)} %get-tuple-element.342), channel_id=1, replica_groups=mesh['dp'=16,'row'=4,'col'=2] {'dp'}, use_global_device_ids=true, to_apply=%region_24.25 | all-reduce | flops 768 | bytes 3072 | tf_op jit(solution)/shard_map/psum | solution.py:321
  652.8 29.2 %all-reduce.4.cloned.1.call-done = (bf16[384,768]{1,0:T(8,128)(2,1)}, bf16[384,768]{1,0:T(8,128)(2,1)}, bf16[768,384]{1,0:T(8,128)(2,1)}, bf16[384,2048]{1,0:T(8...) async-done(((bf16[384,768]{1,0:T(8,128)(2,1)}, bf16[384,768]{1,0:T(8,128)(2,1)}, bf16[768,384]{1,0:T(8,128)(2,1)}, bf16[384,2048]{1,0:T(8,128)(2,1)}, ...) | async-done | bytes 6488080 | tf_op jit(solution)/shard_map/psum | solution.py:322
  (279 shorter events, 228.9 us)
Async XLA Ops:
  7.2 71.5 %all-gather.10.cloned.1.call-start = ((), (), s32[]{:S(2)}) async-start(), calls=%async_computation.19 | async-start | bytes 3932160 | tf_op jit(solution)/shard_map/all_gather | solution.py:108
  33.9 14.7 %all-to-all-start.2 = ((bf16[384,4,192]{0,2,1:T(8,128)(2,1)}), bf16[384,4,192]{0,2,1:T(8,128)(2,1)S(1)}, u32[]{:S(2)}, u32[]{:S(2)}) async-start(bf16[384,4,192]{0,2,1:T(8,128)(2,1)} %bitcast.20), calls=%async_computation.2 | async-start | bytes 1179648 | tf_op jit(solution)/shard_map/all_to_all | solution.py:110
  48.6 19.6 %all-to-all-start.3 = ((bf16[384,4,192]{0,2,1:T(8,128)(2,1)}), bf16[384,4,192]{0,2,1:T(8,128)(2,1)S(1)}, u32[]{:S(2)}, u32[]{:S(2)}) async-start(bf16[384,4,192]{0,2,1:T(8,128)(2,1)} %bitcast.28), calls=%async_computation.3 | async-start | bytes 1179648 | tf_op jit(solution)/shard_map/all_to_all | solution.py:111
  52.1 76.1 %all-gather.12.cloned.1.call-start = ((), (), s32[]{:S(2)}) async-start(), calls=%async_computation.20 | async-start | bytes 1966080 | tf_op jit(solution)/shard_map/all_gather | solution.py:121
  102.4 172.9 %all-gather.16.cloned.1.call-start = ((), (), s32[]{:S(2)}) async-start(), calls=%async_computation.22 | async-start | bytes 3932160 | tf_op jit(solution)/shard_map/all_gather | solution.py:130
  121.7 159.1 %all-gather.14.cloned.1.call-start = ((), (), s32[]{:S(2)}) async-start(), calls=%async_computation.21 | async-start | bytes 3932160 | tf_op jit(solution)/shard_map/all_gather | solution.py:108
  157.1 245.5 %copy-start.27 = (f32[512]{0:T(512)}, f32[512]{0:T(512)S(1)}, u32[]{:S(2)}) copy-start(f32[512]{0:T(512)S(1)} %add_rsqrt_fusion) | copy-start | bytes 6148
  182.3 33.2 %all-to-all-start.11 = ((bf16[4,512,384]{2,1,0:T(8,128)(2,1)}), bf16[4,512,384]{2,1,0:T(8,128)(2,1)S(1)}, u32[]{:S(2)}, u32[]{:S(2)}) async-start(bf16[4,512,384]{2,1,0:T(8,128)(2,1)} %bitcast.490), calls=%async_computation.11 | async-start | bytes 3145728 | tf_op jit(solution)/shard_map/all_to_all | solution.py:131
  215.5 32.7 %all-to-all-start.7 = ((bf16[384,4,512]{0,2,1:T(8,128)(2,1)}), bf16[384,4,512]{0,2,1:T(8,128)(2,1)}, u32[]{:S(2)}, u32[]{:S(2)}) async-start(bf16[384,4,512]{0,2,1:T(8,128)(2,1)} %bitcast.476), calls=%async_computation.7 | async-start | bytes 3145728 | tf_op jit(solution)/shard_map/all_to_all | solution.py:110
  248.2 24.5 %all-to-all-start.8 = ((bf16[384,4,512]{0,2,1:T(8,128)(2,1)}), bf16[384,4,512]{0,2,1:T(8,128)(2,1)}, u32[]{:S(2)}, u32[]{:S(2)}) async-start(bf16[384,4,512]{0,2,1:T(8,128)(2,1)} %bitcast.475), calls=%async_computation.8 | async-start | bytes 3145728 | tf_op jit(solution)/shard_map/all_to_all | solution.py:111
  252.6 118.0 %all-gather.18.cloned.1.call-start = ((), (), s32[]{:S(2)}) async-start(), calls=%async_computation.23 | async-start | bytes 10485760 | tf_op jit(solution)/shard_map/all_gather | solution.py:53
  290.2 80.4 %copy-start.11 = (bf16[384,2048]{1,0:T(8,128)(2,1)S(1)}, bf16[384,2048]{1,0:T(8,128)(2,1)}, u32[]{:S(2)}) copy-start(bf16[384,2048]{1,0:T(8,128)(2,1)} %param.21) | copy-start | bytes 4718596
  290.2 167.6 %all-gather.20.cloned.1.call-start = ((), (), s32[]{:S(2)}) async-start(), calls=%async_computation.24 | async-start | bytes 3932160 | tf_op jit(solution)/shard_map/all_gather | solution.py:130
  418.7 16.1 %all-to-all-start.15 = ((bf16[4,192,384]{2,1,0:T(8,128)(2,1)}), bf16[4,192,384]{2,1,0:T(8,128)(2,1)}, u32[]{:S(2)}, u32[]{:S(2)}) async-start(bf16[4,192,384]{2,1,0:T(8,128)(2,1)} %bitcast.78), calls=%async_computation.15 | async-start | bytes 1179648 | tf_op jit(solution)/shard_map/all_to_all | solution.py:131
  422.9 91.1 %all-gather.24.cloned.1.call-start = ((), (), s32[]{:S(2)}) async-start(), calls=%async_computation.26 | async-start | bytes 5242880 | tf_op jit(solution)/shard_map/all_gather | solution.py:121
  439.4 110.8 %all-gather.22.cloned.1.call-start = ((), (), s32[]{:S(2)}) async-start(), calls=%async_computation.25 | async-start | bytes 3932160 | tf_op jit(solution)/shard_map/all_gather | solution.py:53
  513.7 168.3 %all-reduce.4.cloned.1.call-start = ((), (), s32[]{:S(2)}) async-start(), calls=%async_computation.27 | async-start | bytes 12976128 | tf_op jit(solution)/shard_map/psum | solution.py:322
  560.6 17.1 %all-to-all-start.16 = ((bf16[2,1,512,384]{3,2,1,0:T(8,128)(2,1)}), bf16[2,1,512,384]{3,2,1,0:T(8,128)(2,1)S(1)}, u32[]{:S(2)}, u32[]{:S(2)}) async-start(bf16[2,1,512,384]{3,2,1,0:T(8,128)(2,1)} %bitcast.96), calls=%async_computation.16 | async-start | bytes 1572864 | tf_op jit(solution)/shard_map/all_to_all | solution.py:45
  578.5 16.7 %all-to-all-start.9 = ((bf16[2,1,512,384]{3,2,1,0:T(8,128)(2,1)}), bf16[2,1,512,384]{3,2,1,0:T(8,128)(2,1)}, u32[]{:S(2)}, u32[]{:S(2)}) async-start(bf16[2,1,512,384]{3,2,1,0:T(8,128)(2,1)} %bitcast.51), calls=%async_computation.9 | async-start | bytes 1572864 | tf_op jit(solution)/shard_map/all_to_all | solution.py:45
  582.9 67.2 %copy-start.3 = (bf16[1,512,384]{2,1,0:T(8,128)(2,1)S(1)}, bf16[1,512,384]{2,1,0:T(8,128)(2,1)}, u32[]{:S(2)}) copy-start(bf16[1,512,384]{2,1,0:T(8,128)(2,1)} %param.24) | copy-start | bytes 1179652
  582.9 67.2 %copy-start.28 = (f32[512]{0:T(512)S(1)}, f32[512]{0:T(512)}, u32[]{:S(2)}) copy-start(f32[512]{0:T(512)} %copy-done.27) | copy-start | bytes 6148
  582.9 67.2 %copy-start.33 = (f32[384]{0:T(512)S(1)}, f32[384]{0:T(512)}, u32[]{:S(2)}) copy-start(f32[384]{0:T(512)} %param.20) | copy-start | bytes 4612
  595.8 8.5 %all-to-all-start.18 = ((f32[2,1,768]{2,1,0:T(1,128)}), f32[2,1,768]{2,1,0:T(1,128)S(1)}, u32[]{:S(2)}, u32[]{:S(2)}) async-start(f32[2,1,768]{2,1,0:T(1,128)} %broadcast_in_dim.114), calls=%async_computation.18 | async-start | bytes 12288 | tf_op jit(solution)/shard_map/all_to_all | solution.py:19
  605.0 45.1 %all-to-all-start.17 = ((f32[4,1,512]{2,1,0:T(1,128)}), f32[4,1,512]{2,1,0:T(1,128)S(1)}, u32[]{:S(2)}, u32[]{:S(2)}) async-start(f32[4,1,512]{2,1,0:T(1,128)} %broadcast_in_dim.113), calls=%async_computation.17 | async-start | bytes 16384 | tf_op jit(solution)/shard_map/all_to_all | solution.py:19
  (42 other events, 503.4 us)
Sparse Core Ops, SparseCore 0:
  32.9 45.6 all-gather.9
  102.5 25.6 all-gather.11
  129.9 49.3 all-gather.15
  182.4 56.6 all-gather.13
  290.3 80.1 all-gather.17
  418.8 38.9 all-gather.19
  460.0 44.7 all-gather.23
  513.8 36.2 all-gather.21
  555.5 126.3 all-reduce.3
where the time goes:
time: 711 us; the launch traced here: 699 us
  waiting for transfers between devices  286 us (40%)
  blocking collectives  173 us (24%)
  matrix products  86.5 us (12%)
  local copies, waits for them, and re-layouts  49.4 us (7%)
  other arithmetic  41.7 us (6%)
  starting transfers between devices  39.4 us (6%)
  between operations  14.9 us (2%)
  loops' own time  7.95 us (1%)
    all_gather x2, waiting for transfers between devices, gather_turned(): result = lax.all_gather(both, axis, axis=0, tiled=True)  98.1 us
    all_to_all x7, blocking collectives, from_everyone(): return lax.all_to_all(copies, axis, split_axis=0, concat_axis=0, tiled=True)  95.1 us
    psum x1, blocking collectives, body(): lax.psum(gain_totals[0].astype(jnp.bfloat16), 'dp').astype(jnp.float32)  40.6 us
    all_to_all x2, waiting for transfers between devices, back_out(): lax.all_to_all(weight_matrix, 'row', split_axis=0, concat_axis=1, tiled=T...  38.8 us
    all_to_all x2, blocking collectives, summed_on_arrival(): lax.all_to_all(cut_along(value, dim, count), axis, 0, 0, tiled=True)  37.1 us
    all_to_all x2, waiting for transfers between devices, project_in(): lax.all_to_all(leading_factor, 'row', split_axis=1, concat_axis=0, tiled=...  34.2 us
    all_to_all x2, waiting for transfers between devices, project_in(): lax.all_to_all(trailing_factor, 'row', split_axis=1, concat_axis=0, tiled...  31.3 us
    psum x1, waiting for transfers between devices, body(): lax.psum(grad_w_query.astype(jnp.bfloat16), 'dp').astype(jnp.float32)  29.2 us
  transfers between devices with their start and end apart: 19, of which 15 were waited for; matrix products, arithmetic and copies ran while one was open for 17% of the time, Pallas kernels for 0%

commit v1 on v0

v1 whole, which is shorter than its diff:
```python
import jax
import jax.numpy as jnp
from jax import lax
from jax.experimental import pallas as pl
from jax.experimental.pallas import tpu as pltpu
from jax.sharding import Mesh
from jax.sharding import PartitionSpec as P

D = 1536
HD = 96
HALF = HD // 2
EPS = 1e-05
THETA = 100000.0
NEGATIVE = -1e30
SCALE = HD**-0.5
LOG2E = 1.4426950408889634
F32 = jnp.float32
BF16 = jnp.bfloat16
QUARTER = 256
YS = ("yhi", "ylo")


def dot(a, b, dims):
    return lax.dot_general(a, b, (dims, ((), ())), preferred_element_type=F32)


NN = ((1,), (0,))
NT = ((1,), (1,))
TN = ((0,), (0,))


def swap(value, axis, step=1):
    count = lax.axis_size(axis)
    return lax.ppermute(value, axis, [(i, i ^ step) for i in range(count)])


def from_peers(value, axis):
    return [value] + [swap(value, axis, k) for k in range(1, lax.axis_size(axis))]


def placed(parts, axis):
    count = len(parts)
    if count == 1:
        return parts[0][None]
    me = lax.axis_index(axis)
    out = jnp.zeros((count, *parts[0].shape), parts[0].dtype)
    for k, part in enumerate(parts):
        out = lax.dynamic_update_index_in_dim(out, part, me ^ k, 0)
    return out


def sum_scatter(value, axis):
    count = lax.axis_size(axis)
    me = lax.axis_index(axis)

    def entry(k):
        return lax.dynamic_index_in_dim(value, me ^ k, 0, keepdims=False)

    total = entry(0).astype(F32)
    got = [swap(entry(k).astype(BF16), axis, k) for k in range(1, count)]
    for g in got:
        total = total + g.astype(F32)
    return total


def gather_dp(first, second):
    a = placed(from_peers(first, "x"), "x")
    b = placed(from_peers(second, "z"), "z")
    a = placed(from_peers(a, "z"), "z")
    b = placed(from_peers(b, "x"), "x")
    return jnp.swapaxes(a, 0, 1), b


def scatter_dp(first, second):
    a = sum_scatter(first, "x").astype(BF16)
    b = sum_scatter(jnp.swapaxes(second, 0, 1), "z").astype(BF16)
    a = sum_scatter(a, "z").astype(BF16)
    b = sum_scatter(b, "x").astype(BF16)
    return a, b


def over_y(value):
    return lax.all_to_all(value, YS, 0, 0, tiled=True)


def gather_y(value):
    return over_y(jnp.broadcast_to(value[None], (4, *value.shape)))


def small_sum(value):
    for axis in ("core", "ylo", "yhi", "x", "z"):
        parts = from_peers(value, axis)
        value = sum(parts[1:], parts[0])
    return value


def key_blocks(block):
    return (0, 2) if block == 0 else (0, 1, 2, 3)


def allowed_keys(offs_ref, key, place, low):
    at = offs_ref[key] + lax.broadcasted_iota(jnp.int32, (QUARTER, place.shape[1]), 0)
    return (at >= low) & (at <= place)


def two_heads(ref, group, block):
    lanes = pl.ds(block * QUARTER, QUARTER)
    return jnp.concatenate(
        [ref[pl.ds((2 * group + h) * HD, HD), lanes] for h in range(2)], axis=1
    )


def twice(ref, block):
    row = ref[:, pl.ds(block * QUARTER, QUARTER)]
    return jnp.concatenate([row, row], axis=1)


def forward_kernel(offs_ref, q_ref, own_ref, oth_ref, place_ref, low_ref, out_ref, lse_ref):
    factor = SCALE * LOG2E
    for group in range(2):
        keys = []
        vals = []
        for ref in (own_ref, oth_ref):
            for half in range(2):
                lanes = pl.ds(half * QUARTER, QUARTER)
                keys.append(ref[pl.ds(group * 2 * HD, HD), lanes].T)
                vals.append(ref[pl.ds(group * 2 * HD + HD, HD), lanes])
        for block in range(2):
            q = two_heads(q_ref, group, block)
            place, low = twice(place_ref, block), twice(low_ref, block)
            scores = []
            for key in key_blocks(block):
                s = dot(keys[key], q, NN)
                scores.append(jnp.where(allowed_keys(offs_ref, key, place, low), s, NEGATIVE))
            peak = scores[0].max(axis=0, keepdims=True)
            for s in scores[1:]:
                peak = jnp.maximum(peak, s.max(axis=0, keepdims=True))
            shift = peak * factor
            total = jnp.zeros_like(peak)
            acc = jnp.zeros((HD, 2 * QUARTER), F32)
            for key, s in zip(key_blocks(block), scores):
                p = jnp.exp2(s * factor - shift)
                total = total + p.sum(axis=0, keepdims=True)
                acc = acc + dot(vals[key], p.astype(BF16), NN)
            acc = (acc / total).astype(BF16)
            lse = shift + jnp.log2(total)
            for h in range(2):
                lanes = pl.ds(block * QUARTER, QUARTER)
                cut = slice(h * QUARTER, (h + 1) * QUARTER)
                out_ref[pl.ds((2 * group + h) * HD, HD), lanes] = acc[:, cut]
                lse_ref[pl.ds(2 * group + h, 1), lanes] = lse[:, cut]


def backward_kernel(
    offs_ref, q_ref, own_ref, oth_ref, do_ref, o_ref, lse_ref, place_ref, low_ref,
    dq_ref, down_ref, doth_ref,
):
    factor = SCALE * LOG2E
    for group in range(2):
        keys, vals, keyst = [], [], []
        for ref in (own_ref, oth_ref):
            for half in range(2):
                lanes = pl.ds(half * QUARTER, QUARTER)
                kt = ref[pl.ds(group * 2 * HD, HD), lanes]
                keyst.append(kt)
                keys.append(kt.T)
                vals.append(ref[pl.ds(group * 2 * HD + HD, HD), lanes].T)
        dks = [jnp.zeros((HD, QUARTER), F32) for _ in range(4)]
        dvs = [jnp.zeros((HD, QUARTER), F32) for _ in range(4)]
        for block in range(2):
            lanes = pl.ds(block * QUARTER, QUARTER)
            q = two_heads(q_ref, group, block)
            do = two_heads(do_ref, group, block)
            o = two_heads(o_ref, group, block)
            place, low = twice(place_ref, block), twice(low_ref, block)
            lse = jnp.concatenate(
                [lse_ref[pl.ds(2 * group + h, 1), lanes] for h in range(2)], axis=1
            )
            delta = (do.astype(F32) * o.astype(F32)).sum(axis=0, keepdims=True)
            dq = jnp.zeros((HD, 2 * QUARTER), F32)
            for key in key_blocks(block):
                s = dot(keys[key], q, NN)
                p = jnp.exp2(s * factor - lse)
                p = jnp.where(allowed_keys(offs_ref, key, place, low), p, 0.0)
                dp = dot(vals[key], do, NN)
                ds = (p * (dp - delta)).astype(BF16)
                dvs[key] = dvs[key] + dot(do, p.astype(BF16), NT)
                dks[key] = dks[key] + dot(q, ds, NT)
                dq = dq + dot(keyst[key], ds, NN)
            dq = dq * SCALE
            for h in range(2):
                cut = slice(h * QUARTER, (h + 1) * QUARTER)
                dq_ref[pl.ds((2 * group + h) * HD, HD), lanes] = dq[:, cut]
        for i, ref in enumerate((down_ref, doth_ref)):
            for half in range(2):
                lanes = pl.ds(half * QUARTER, QUARTER)
                rows = group * 2 * HD
                ref[pl.ds(rows, HD), lanes] = (dks[2 * i + half] * SCALE).astype(ref.dtype)
                ref[pl.ds(rows + HD, HD), lanes] = dvs[2 * i + half].astype(ref.dtype)


def vmem():
    return pl.BlockSpec(memory_space=pltpu.VMEM)


def attend(offs, queries, own, other, place, low):
    n, length = queries.shape
    return pl.pallas_call(
        forward_kernel,
        out_shape=(
            jax.ShapeDtypeStruct((n, length), BF16),
            jax.ShapeDtypeStruct((n // HD, length), F32),
        ),
        in_specs=[pl.BlockSpec(memory_space=pltpu.SMEM)] + [vmem()] * 5,
        out_specs=(vmem(), vmem()),
        compiler_params=pltpu.CompilerParams(vmem_limit_bytes=48 << 20),
        cost_estimate=pl.CostEstimate(
            flops=4 * 4 * HD * QUARTER * QUARTER * 6, bytes_accessed=4 << 20, transcendentals=1 << 20
        ),
        name="attend_forward",
    )(offs, queries, own, other, place, low)


def attend_back(offs, queries, own, other, grads, outs, lse, place, low):
    n, length = queries.shape
    return pl.pallas_call(
        backward_kernel,
        out_shape=(
            jax.ShapeDtypeStruct((n, length), F32),
            jax.ShapeDtypeStruct((n, length), F32),
            jax.ShapeDtypeStruct((n, length), BF16),
        ),
        in_specs=[pl.BlockSpec(memory_space=pltpu.SMEM)] + [vmem()] * 8,
        out_specs=(vmem(), vmem(), vmem()),
        compiler_params=pltpu.CompilerParams(vmem_limit_bytes=48 << 20),
        cost_estimate=pl.CostEstimate(
            flops=10 * 4 * HD * QUARTER * QUARTER * 6, bytes_accessed=6 << 20, transcendentals=1 << 20
        ),
        name="attend_backward",
    )(offs, queries, own, other, grads, outs, lse, place, low)


def rotate(values, cosine, sine, sign):
    front, behind = values[:, 0], values[:, 1]
    return jnp.stack(
        [front * cosine - sign * behind * sine, behind * cosine + sign * front * sine], axis=1
    )


def body(tokens, gain1, w_query, w_keyval, w_out, gain2, w_gate, w_up, w_down, grad_out, segments):
    core, yh, yl = lax.axis_index("core"), lax.axis_index("yhi"), lax.axis_index("ylo")
    nx, nz = lax.axis_size("x"), lax.axis_size("z")
    ndp = nx * nz
    dp = lax.axis_index("x") * nz + lax.axis_index("z")
    y = 2 * yh + yl
    mine = core ^ yh
    shard = D // 4

    def pick(first_is_mine, own, other):
        return jnp.where(first_is_mine, own, other), jnp.where(first_is_mine, other, own)

    def whole_rows(value):
        own = lax.dynamic_slice_in_dim(value, mine * QUARTER, QUARTER, 0)
        other = lax.dynamic_slice_in_dim(value, (1 - mine) * QUARTER, QUARTER, 0)
        pair = jnp.stack(pick(core == 0, own, swap(other, "core")))
        got = gather_y(pair).reshape(2, 2, 2, QUARTER, shard)
        return got.transpose(0, 3, 1, 2, 4).reshape(2 * QUARTER, D)

    def exchanged(slab):
        send = lax.dynamic_index_in_dim(slab, 1 - yl, 0, keepdims=False)
        keep = lax.dynamic_index_in_dim(slab, yl, 0, keepdims=False)
        return pick(yl == 0, keep, swap(send, "ylo"))

    def both_cores(left, right):
        pair = jnp.stack([left, right])
        first, second = pick(core == 0, pair, swap(pair, "core"))
        return jnp.concatenate([first[0], second[0], first[1], second[1]], axis=1)

    def part_of(value, dim):
        size = value.shape[dim] // ndp
        return lax.dynamic_slice_in_dim(value, dp * size, size, dim)

    def rows_first(weight):
        return weight.reshape(shard, 2, -1).transpose(1, 2, 0)

    x_rows = whole_rows(tokens[0])

    wide = jnp.concatenate([rows_first(w_query), rows_first(w_keyval)], axis=1)
    left, right = gather_dp(*exchanged(part_of(wide, 1)))
    w_qkv = both_cores(left.reshape(-1, shard), right.reshape(-1, shard))

    piece = gather_y(part_of(w_out, 0))
    piece = piece.reshape(2, 2, *piece.shape[1:])
    left, right = gather_dp(piece[:, 0], piece[:, 1])

    def head_rows(v):
        return v.transpose(2, 0, 1, 3, 4).reshape(-1, shard)

    w_o = both_cores(head_rows(left), head_rows(right))
    w_o_mine = lax.dynamic_slice_in_dim(w_o, y * shard, shard, 0)

    def hidden_slab(weight):
        units = weight.shape[0] // (2 * ndp)
        return part_of(weight, 0).reshape(2, units, shard)

    slabs = [hidden_slab(w_gate.T), hidden_slab(w_up.T), hidden_slab(w_down)]
    units = slabs[0].shape[1]
    left, right = gather_dp(*exchanged(jnp.concatenate(slabs, axis=1)))

    def hidden_rows(v, k):
        return v.reshape(ndp, 3, units, shard)[:, k].reshape(-1, shard)

    w_g, w_u, w_d = [both_cores(hidden_rows(left, k), hidden_rows(right, k)) for k in range(3)]

    gains = gather_small(gain1, gain2)
    gain1, gain2 = gains[0][None, :], gains[1][None, :]

    ids = segments[0]
    low_all = jnp.sum((ids[None, :] < ids[:, None]).astype(jnp.int32), axis=1)
    low = jnp.concatenate(
        [
            lax.dynamic_slice_in_dim(low_all, core * QUARTER, QUARTER),
            lax.dynamic_slice_in_dim(low_all, (3 - core) * QUARTER, QUARTER),
        ]
    )
    step = jnp.arange(QUARTER, dtype=jnp.int32)
    place = jnp.concatenate([core * QUARTER + step, (3 - core) * QUARTER + step])
    rates = THETA ** (-jnp.arange(HALF, dtype=F32) * 2.0 / HD)
    angles = rates[:, None] * (place - low).astype(F32)[None, :]
    cosine, sine = jnp.cos(angles), jnp.sin(angles)
    place, low = place[None, :], low[None, :]
    offs = (jnp.stack([core, 3 - core, 1 - core, 2 + core]) * QUARTER).astype(jnp.int32)

    inputs = x_rows.astype(F32)
    inverse_one = lax.rsqrt(jnp.mean(inputs * inputs, axis=-1, keepdims=True) + EPS)
    normed_one = inputs * inverse_one
    h_one = (normed_one * gain1).astype(BF16)
    raw = dot(w_qkv, h_one, NT)
    queries = rotate(raw[:shard].reshape(4, 2, HALF, -1), cosine, sine, 1.0)
    queries = queries.astype(BF16).reshape(shard, -1)
    keyval = raw[shard:].reshape(2, 2, 2, HALF, -1)
    keys = rotate(keyval[:, 0], cosine, sine, 1.0)
    keyval = jnp.stack([keys, keyval[:, 1]], axis=1).astype(BF16).reshape(shard, -1)
    keyval_other = swap(keyval, "core")
    heads, lse = attend(offs, queries, keyval, keyval_other, place, low)
    heads_all = gather_y(heads).reshape(-1, heads.shape[1])
    mixed = inputs + dot(heads_all, w_o, TN)

    inverse_two = lax.rsqrt(jnp.mean(mixed * mixed, axis=-1, keepdims=True) + EPS)
    h_two = (mixed * inverse_two * gain2).astype(BF16)
    gate = dot(h_two, w_g, NT)
    upward = dot(h_two, w_u, NT)
    sigma = jax.nn.sigmoid(gate)
    hidden = (gate * sigma * upward).astype(BF16)
    top = whole_rows(grad_out[0])
    grad_hidden = dot(top, w_d, NT)
    grad_gate = (grad_hidden * upward * sigma * (1.0 + gate * (1.0 - sigma))).astype(BF16)
    grad_up = (grad_hidden * gate * sigma).astype(BF16)
    part = dot(grad_gate, w_g, NN) + dot(grad_up, w_u, NN)
    got = over_y(part.astype(BF16).reshape(4, 128, D))
    grad_two = got.astype(F32).sum(axis=0)

    def my_rows(value):
        return lax.dynamic_slice_in_dim(value, y * 128, 128, 0)

    inv_two = my_rows(inverse_two)
    normed_two = my_rows(mixed) * inv_two
    gain2_part = (grad_two * normed_two).sum(axis=0)
    scaled = grad_two * gain2
    inner = jnp.mean(scaled * normed_two, axis=-1, keepdims=True)
    grad_mixed = my_rows(top).astype(F32) + inv_two * (scaled - normed_two * inner)
    residual = gather_y(grad_mixed.astype(BF16)).reshape(-1, D)

    grad_heads = dot(w_o_mine, residual, NT).astype(BF16)
    dq, dkv, dkv_other = attend_back(
        offs, queries, keyval, keyval_other, grad_heads, heads, lse, place, low
    )
    dkv = dkv + swap(dkv_other, "core").astype(F32)
    dq = rotate(dq.reshape(4, 2, HALF, -1), cosine, sine, -1.0).reshape(shard, -1)
    dkv = dkv.reshape(2, 2, 2, HALF, -1)
    dk = rotate(dkv[:, 0], cosine, sine, -1.0)
    dkv = jnp.stack([dk, dkv[:, 1]], axis=1).reshape(shard, -1)
    grad_raw = jnp.concatenate([dq, dkv]).astype(BF16)
    part = dot(grad_raw, w_qkv, TN)
    gain1_part = (part * normed_one).sum(axis=0)
    inner = (part * normed_one * gain1).sum(axis=-1)
    got = over_y(blocks(part.astype(BF16)))
    inner = over_y(jnp.broadcast_to(inner.reshape(2, 1, QUARTER), (2, 2, QUARTER)).reshape(4, -1))
    inner = inner.sum(axis=0)[:, None] / D

    def my_block(value):
        return lax.dynamic_slice(value, (yh * QUARTER, yl * D // 2), (QUARTER, D // 2))

    gain1_mine = lax.dynamic_slice(gain1, (0, yl * D // 2), (1, D // 2))
    inv_one = lax.dynamic_slice_in_dim(inverse_one, yh * QUARTER, QUARTER, 0)
    normed_block = my_block(x_rows).astype(F32) * inv_one
    scaled = got.astype(F32).sum(axis=0) * gain1_mine
    grad_in = my_block(residual).astype(F32) + inv_one * (scaled - normed_block * inner)

    def to_home(block):
        own = lax.dynamic_slice_in_dim(block, core * shard, shard, 1)
        other = lax.dynamic_slice_in_dim(block, (1 - core) * shard, shard, 1)
        return jnp.concatenate(pick(mine == 0, own, swap(other, "core")))

    grad_in = to_home(grad_in)
    mlp = over_y(blocks(dot(hidden, w_d, NN).astype(BF16)))
    output = to_home((my_block(mixed) + mlp.astype(F32).sum(axis=0)).astype(BF16))

    def for_core(value, who):
        cut = value.reshape(-1, 2, 2, shard)
        return lax.dynamic_index_in_dim(cut, who, 2, keepdims=False).reshape(-1, 2 * shard)

    def weight_grad(left_dims, rows, columns):
        send = dot(rows, for_core(columns, 1 - core), left_dims).astype(BF16)
        return dot(rows, for_core(columns, core), left_dims) + swap(send, "core").astype(F32)

    def reduced(total):
        total = total.astype(BF16)
        cut = total.reshape(nx, nz, -1, 2 * shard)
        left, right = scatter_dp(cut[..., :shard], cut[..., shard:])
        send = jnp.where(yl == 0, right, left)
        keep = jnp.where(yl == 0, left, right)
        first, second = gather_dp(*pick(yl == 0, keep, swap(send, "ylo")))
        return first.reshape(ndp, -1, shard), second.reshape(ndp, -1, shard)

    grad_d = weight_grad(TN, hidden, top)
    grad_g = weight_grad(TN, grad_gate, h_two)
    grad_u = weight_grad(TN, grad_up, h_two)
    total = jnp.stack([v.reshape(ndp, units, -1) for v in (grad_g, grad_u, grad_d)], axis=1)
    first, second = reduced(total.reshape(-1, 2 * shard))

    def hidden_grad(k):
        cut = [v.reshape(ndp, 3, units, shard)[:, k] for v in (first, second)]
        return jnp.stack(cut, axis=1).reshape(-1, shard).astype(F32)

    grad_w_gate, grad_w_up, grad_w_down = hidden_grad(0).T, hidden_grad(1).T, hidden_grad(2)

    grad_o = weight_grad(NN, heads, residual)
    grad_qkv = weight_grad(NN, grad_raw, h_one)
    total = jnp.concatenate([grad_qkv, grad_o])
    first, second = reduced(total)
    both = jnp.stack([v.reshape(-1, shard) for v in (first, second)]).astype(F32)
    grad_w_query = both[:, :shard].reshape(-1, shard).T
    grad_w_keyval = both[:, shard : 2 * shard].reshape(-1, shard).T
    grad_w_out = both[:, 2 * shard :].reshape(-1, shard)

    gains = small_sum(jnp.stack([gain1_part, gain2_part]))
    home = (yl * 2 + core) * shard
    gains = lax.dynamic_slice(gains, (0, home), (2, shard))
    return (
        output[None],
        grad_in[None],
        gains[0],
        grad_w_query,
        grad_w_keyval,
        grad_w_out,
        gains[1],
        grad_w_gate,
        grad_w_up,
        grad_w_down,
    )


def blocks(value):
    return value.reshape(2, QUARTER, 2, D // 2).transpose(0, 2, 1, 3).reshape(4, QUARTER, D // 2)


def gather_small(gain1, gain2):
    pair = jnp.stack([gain1, gain2])
    first = placed(from_peers(pair, "core"), "core")
    both = placed(from_peers(first, "ylo"), "ylo")
    return both.transpose(2, 0, 1, 3).reshape(2, D)


def solution(mesh):
    dp = mesh.shape["dp"]
    side = int(round(dp**0.5))
    fine = Mesh(
        mesh.devices.reshape(side, dp // side, 2, 2, 2), ("x", "z", "ylo", "core", "yhi")
    )
    seq, row, col = ("x", "z"), ("ylo", "core"), "yhi"
    return jax.shard_map(
        body,
        mesh=fine,
        in_specs=(
            P(seq, col, row),
            P(row),
            P(row, col),
            P(row, col),
            P(col, row),
            P(row),
            P(row, col),
            P(row, col),
            P(col, row),
            P(seq, col, row),
            P(seq, None),
        ),
        out_specs=(
            P(seq, col, row),
            P(seq, col, row),
            P(row),
            P(row, col),
            P(row, col),
            P(col, row),
            P(row),
            P(row, col),
            P(row, col),
            P(col, row),
        ),
        check_vma=False,
    )
```

time: 711 us -> 636 us (0.89)
  blocking collectives: 173 us -> 0 us
  waiting for transfers between devices: 286 us -> 137 us
  starting transfers between devices: 39.4 us -> 184 us
  local copies, waits for them, and re-layouts: 49.4 us -> 171 us
  matrix products: 86.5 us -> 57 us
  other arithmetic: 41.7 us -> 63.2 us
  between operations: 14.9 us -> 3.63 us
  Pallas kernels: 0 us -> 8.85 us
  loops' own time: 7.95 us -> 0 us
    ppermute x0 -> x115, starting transfers between devices: none -> 145 us  [swap(): return lax.ppermute(value, axis, [(i, i ^ step) for i in range(count)])]
    all_gather x8 -> x0, waiting for transfers between devices: 133 us -> none  [the longest x2 98.1 us: gather_turned(): result = lax.all_gather(both, axis, axis=0, tiled=True)]
    all_to_all x9 -> x0, blocking collectives: 132 us -> none  [the longest x7 95.1 us: from_everyone(): return lax.all_to_all(copies, axis, split_axis=0, concat_axis=0, tiled=True)]
    ppermute x0 -> x115, waiting for transfers between devices: none -> 131 us  [swap(): return lax.ppermute(value, axis, [(i, i ^ step) for i in range(count)])]
    all_to_all x10 -> x9, waiting for transfers between devices: 124 us -> 5.29 us  [over_y(): return lax.all_to_all(value, YS, 0, 0, tiled=True)]
    psum x1 -> x0, blocking collectives: 40.6 us -> none  [body(): lax.psum(gain_totals[0].astype(jnp.bfloat16), 'dp').astype(jnp.float32)]
    dynamic_slice x8 -> x19, local copies, waits for them, and re-layouts: 3.96 us -> 35.4 us  [the longest x10 29.8 us: for_core(): lax.dynamic_index_in_dim(cut, who, 2, keepdims=False).reshape(-1, 2 * shard)]
    dot_general x32 -> x20, matrix products: 86.5 us -> 57 us  [dot(): return lax.dot_general(a, b, (dims, ((), ())), preferred_element_type=F32)]
  transfers between devices with their start and end apart: 19 -> 124, of which waited for: 15 -> 45; matrix products, arithmetic and copies ran while one was open for 17% -> 38% of each run, Pallas kernels for 0% -> 1%
where the time goes in v1:
time: 636 us; the launch traced here: 625 us
  starting transfers between devices  184 us (29%)
  local copies, waits for them, and re-layouts  171 us (27%)
  waiting for transfers between devices  137 us (22%)
  other arithmetic  63.2 us (10%)
  matrix products  57 us (9%)
  Pallas kernels  8.85 us (1%)
    ppermute x115, starting transfers between devices, swap(): return lax.ppermute(value, axis, [(i, i ^ step) for i in range(count)])  145 us
    ppermute x115, waiting for transfers between devices, swap(): return lax.ppermute(value, axis, [(i, i ^ step) for i in range(count)])  131 us
    dot_general x20, matrix products, dot(): return lax.dot_general(a, b, (dims, ((), ())), preferred_element_type=F32)  57 us
    all_to_all x9, starting transfers between devices, over_y(): return lax.all_to_all(value, YS, 0, 0, tiled=True)  39.4 us
    dynamic_slice x10, local copies, waits for them, and re-layouts, for_core(): lax.dynamic_index_in_dim(cut, who, 2, keepdims=False).reshape(-1, 2 * shard)  29.8 us
    unnamed x232, local copies, waits for them, and re-layouts  28 us
    dynamic_update_slice x79, local copies, waits for them, and re-layouts, placed(): out = lax.dynamic_update_index_in_dim(out, part, me ^ k, 0)  27.3 us
  transfers between devices with their start and end apart: 124, of which 45 were waited for; matrix products, arithmetic and copies ran while one was open for 38% of the time, Pallas kernels for 1%

profile of v1, /device:TPU:0, one launch (start us, length us, event | category | flops | bytes accessed | tf_op | source)
XLA Modules:
  0.0 624.6 jit_solution(6081871931771705323)
XLA Ops:
  11.1 4.2 all-to-all-start.2
  81.7 4.4 collective-permute-done.20
  146.9 5.0 collective-permute-done.41
  152.0 12.5 %collective-permute-done.42 = bf16[4,192,384]{2,1,0:T(8,128)(2,1)S(1)} collective-permute-done((bf16[4,192,384]{2,1,0:T(8,128)(2,1)}, bf16[4,192,384]{2,1,0:T(8,128)(2,1)S(1)}, u32[]{:S(2)}, u32[]{:S(2)}) %collective-permute-start.42) | collective-permute-done | bytes 589856 | tf_op jit(solution)/shard_map/ppermute | solution.py:34
  168.0 12.4 %collective-permute-done.37 = bf16[4,192,384]{2,1,0:T(8,128)(2,1)S(1)} collective-permute-done((bf16[4,192,384]{2,1,0:T(8,128)(2,1)S(1)}, bf16[4,192,384]{2,1,0:T(8,128)(2,1)S(1)}, u32[]{:S(2)}, u32[]{:S(2)}) %collective-permute-start.37) | collective-permute-done | bytes 589856 | tf_op jit(solution)/shard_map/ppermute | solution.py:34
  184.8 4.8 all-to-all-start.4
  197.6 4.8 reshape.395
  205.0 4.1 all-to-all-done.4
  238.9 4.8 all-to-all-start.1
  265.4 7.4 %multiply_reduce_fusion.1 = (f32[512]{0:T(512)S(1)}, f32[512,1536]{1,0:T(8,128)}) fusion(bf16[1536,512]{1,0:T(8,128)(2,1)} %bitcast.61, bf16[1536,384]{1,0:T(8,128)(2,1)} %copy-done.29, bf16[1536,384]{1,0:T(8,128)(2,1)} %copy-done.30, bf16[1536,384]{1,0:T(8,128)(2,1)S(1)} %get-tuple-element.126, bf16[1536,384]{1,0:T(8,128)(2,1)} %copy-done.31, ...), kind=kOutput, calls=%fused_computation.25 | convolution fusion | flops 2437938688 | bytes 11012096 | tf_op jit(solution)/shard_map/dot_general | solution.py:24
  279.8 4.2 fusion.22
  295.5 4.4 all-to-all-start.5
  299.9 4.9 constant_dynamic-slice_fusion.5
  329.1 4.8 all-to-all-start.3
  363.3 17.1 %collective-permute-done.92 = bf16[4,192,384]{2,1,0:T(8,128)(2,1)} collective-permute-done((bf16[4,192,384]{2,1,0:T(8,128)(2,1)}, bf16[4,192,384]{2,1,0:T(8,128)(2,1)}, u32[]{:S(2)}, u32[]{:S(2)}) %collective-permute-start.92) | collective-permute-done | bytes 589856 | tf_op jit(solution)/shard_map/ppermute | solution.py:34
  384.4 4.6 all-to-all-start.6
  404.2 4.8 collective-permute-done.101
  415.9 5.4 attend_backward.1
  421.6 4.6 reshape_reshape.8
  426.1 6.9 %constant_dynamic-slice_fusion.7 = (bf16[512,2,1,384]{3,2,1,0:T(2,128)(2,1)}, bf16[512,2,1,384]{3,2,1,0:T(2,128)(2,1)}) fusion(bf16[512,2,2,384]{3,2,1,0:T(2,128)(2,1)} %reshape_reshape.8, s32[]{:T(128)S(6)} %select_n.455, s32[]{:T(128)S(6)} %select_n.421), kind=kLoop, calls=%fused_computation.295 | loop fusion | bytes 3145736 | tf_op jit(solution)/shard_map/jit(dynamic_index_in_dim)/dynamic_slice | solution.py:411
  433.0 4.7 copy.292
  495.9 5.0 all-to-all-start.7
  522.3 12.4 %collective-permute-done.114 = bf16[4,192,384]{2,1,0:T(8,128)(2,1)S(1)} collective-permute-done((bf16[4,192,384]{2,1,0:T(8,128)(2,1)}, bf16[4,192,384]{2,1,0:T(8,128)(2,1)S(1)}, u32[]{:S(2)}, u32[]{:S(2)}) %collective-permute-start.114) | collective-permute-done | bytes 589856 | tf_op jit(solution)/shard_map/ppermute | solution.py:34
  538.9 4.3 collective-permute-done.108
  (748 shorter events, 468.8 us)
Async XLA Ops:
  2.5 85.0 %collective-permute-start.48 = (bf16[256,384]{1,0:T(8,128)(2,1)}, bf16[256,384]{1,0:T(8,128)(2,1)}, u32[]{:S(2)}, u32[]{:S(2)}) collective-permute-start(bf16[256,384]{1,0:T(8,128)(2,1)} %dynamic-slice_bitcast_fusion.12), channel_id=1, source_target_pairs={{0,2},{2,0},{1,3},{3,1},{4,6},{6,4},{5,7},{7,5},{8,10},{10,8},{9,1... | collective-permute-start | bytes 589832 | tf_op jit(solution)/shard_map/ppermute | solution.py:34
  4.1 83.5 %collective-permute-start = (bf16[256,384]{1,0:T(8,128)(2,1)}, bf16[256,384]{1,0:T(8,128)(2,1)}, u32[]{:S(2)}, u32[]{:S(2)}) collective-permute-start(bf16[256,384]{1,0:T(8,128)(2,1)} %dynamic-slice_bitcast_fusion.13), channel_id=1, source_target_pairs={{0,2},{2,0},{1,3},{3,1},{4,6},{6,4},{5,7},{7,5},{8,10},{10,8},{9,1... | collective-permute-start | bytes 589832 | tf_op jit(solution)/shard_map/ppermute | solution.py:34
  11.1 42.3 %all-to-all-start.2 = ((bf16[4,48,384]{2,1,0:T(8,128)(2,1)}), bf16[4,48,384]{2,1,0:T(8,128)(2,1)S(1)}, u32[]{:S(2)}, u32[]{:S(2)}) async-start(bf16[4,48,384]{2,1,0:T(8,128)(2,1)} %broadcast_in_dim.365), calls=%async_computation.2 | async-start | bytes 294912 | tf_op jit(solution)/shard_map/all_to_all | solution.py:83
  17.4 36.2 %collective-permute-start.31 = (bf16[192,384]{1,0:T(8,128)(2,1)S(1)}, bf16[192,384]{1,0:T(8,128)(2,1)S(1)}, u32[]{:S(2)}, u32[]{:S(2)}) collective-permute-start(bf16[192,384]{1,0:T(8,128)(2,1)S(1)} %dynamic-slice_bitcast_fusion.20), channel_id=1, source_target_pairs={{0,4},{4,0},{1,5},{5,1},{2,6},{6,2},{3,7},{7,3},{8,12},{12,8},{9,1... | collective-permute-start | bytes 442376 | tf_op jit(solution)/shard_map/ppermute | solution.py:34
  47.6 51.6 %collective-permute-start.11 = (bf16[4,48,384]{2,1,0:T(8,128)(2,1)}, bf16[4,48,384]{2,1,0:T(8,128)(2,1)}, u32[]{:S(2)}, u32[]{:S(2)}) collective-permute-start(bf16[4,48,384]{2,1,0:T(8,128)(2,1)} %constant_dynamic-update-slice_fusion.2), channel_id=1, source_target_pairs={{0,32},{32,0},{64,96},{96,64},{1,33},{33,1},{65,97},{97,65},{2,34}... | collective-permute-start | bytes 442376 | tf_op jit(solution)/shard_map/ppermute | solution.py:34
  51.0 51.7 %collective-permute-start.12 = (bf16[4,48,384]{2,1,0:T(8,128)(2,1)}, bf16[4,48,384]{2,1,0:T(8,128)(2,1)}, u32[]{:S(2)}, u32[]{:S(2)}) collective-permute-start(bf16[4,48,384]{2,1,0:T(8,128)(2,1)} %constant_dynamic-update-slice_fusion.2), channel_id=1, source_target_pairs={{0,64},{32,96},{64,0},{96,32},{1,65},{33,97},{65,1},{97,33},{2,66}... | collective-permute-start | bytes 442376 | tf_op jit(solution)/shard_map/ppermute | solution.py:34
  93.9 89.5 %all-to-all-start = ((bf16[4,2,256,384]{3,2,1,0:T(8,128)(2,1)}), bf16[4,2,256,384]{3,2,1,0:T(8,128)(2,1)S(1)}, u32[]{:S(2)}, u32[]{:S(2)}) async-start(bf16[4,2,256,384]{3,2,1,0:T(8,128)(2,1)} %broadcast_in_dim.339), calls=%async_computation | async-start | bytes 3145728 | tf_op jit(solution)/shard_map/all_to_all | solution.py:83
  134.1 80.3 %collective-permute-start.14 = (bf16[2,768,384]{2,1,0:T(8,128)(2,1)}, bf16[2,768,384]{2,1,0:T(8,128)(2,1)}, u32[]{:S(2)}, u32[]{:S(2)}) collective-permute-start(bf16[2,768,384]{2,1,0:T(8,128)(2,1)} %pad_maximum_fusion.14), channel_id=1, source_target_pairs={{0,2},{2,0},{1,3},{3,1},{4,6},{6,4},{5,7},{7,5},{8,10},{10,8},{9,1... | collective-permute-start | bytes 3538952 | tf_op jit(solution)/shard_map/ppermute | solution.py:34
  167.4 88.9 %collective-permute-start.30 = (bf16[2,1536,384]{2,1,0:T(8,128)(2,1)}, bf16[2,1536,384]{2,1,0:T(8,128)(2,1)}, u32[]{:S(2)}, u32[]{:S(2)}) collective-permute-start(bf16[2,1536,384]{2,1,0:T(8,128)(2,1)} %pad_maximum_fusion.6), channel_id=1, source_target_pairs={{0,2},{2,0},{1,3},{3,1},{4,6},{6,4},{5,7},{7,5},{8,10},{10,8},{9,1... | collective-permute-start | bytes 7077896 | tf_op jit(solution)/shard_map/ppermute | solution.py:34
  190.9 61.3 %collective-permute-start.44 = (bf16[2,1024,384]{2,1,0:T(8,128)(2,1)}, bf16[2,1024,384]{2,1,0:T(8,128)(2,1)}, u32[]{:S(2)}, u32[]{:S(2)}) collective-permute-start(bf16[2,1024,384]{2,1,0:T(8,128)(2,1)} %pad_maximum_fusion.8), channel_id=1, source_target_pairs={{0,2},{2,0},{1,3},{3,1},{4,6},{6,4},{5,7},{7,5},{8,10},{10,8},{9,1... | collective-permute-start | bytes 4718600 | tf_op jit(solution)/shard_map/ppermute | solution.py:34
  192.8 50.8 %collective-permute-start.46 = (bf16[2,1024,384]{2,1,0:T(8,128)(2,1)}, bf16[2,1024,384]{2,1,0:T(8,128)(2,1)}, u32[]{:S(2)}, u32[]{:S(2)}) collective-permute-start(bf16[2,1024,384]{2,1,0:T(8,128)(2,1)} %pad_maximum_fusion.10), channel_id=1, source_target_pairs={{0,2},{2,0},{1,3},{3,1},{4,6},{6,4},{5,7},{7,5},{8,10},{10,8},{9,1... | collective-permute-start | bytes 4718600 | tf_op jit(solution)/shard_map/ppermute | solution.py:34
  194.2 49.5 %collective-permute-start.45 = (bf16[2,1024,384]{2,1,0:T(8,128)(2,1)}, bf16[2,1024,384]{2,1,0:T(8,128)(2,1)}, u32[]{:S(2)}, u32[]{:S(2)}) collective-permute-start(bf16[2,1024,384]{2,1,0:T(8,128)(2,1)} %pad_maximum_fusion.9), channel_id=1, source_target_pairs={{0,2},{2,0},{1,3},{3,1},{4,6},{6,4},{5,7},{7,5},{8,10},{10,8},{9,1... | collective-permute-start | bytes 4718600 | tf_op jit(solution)/shard_map/ppermute | solution.py:34
  295.5 33.6 %all-to-all-start.5 = ((bf16[4,128,1536]{2,1,0:T(8,128)(2,1)}), bf16[4,128,1536]{2,1,0:T(8,128)(2,1)}, u32[]{:S(2)}, u32[]{:S(2)}) async-start(bf16[4,128,1536]{2,1,0:T(8,128)(2,1)} %bitcast.638), calls=%async_computation.5 | async-start | bytes 3145728 | tf_op jit(solution)/shard_map/all_to_all | solution.py:83
  350.8 29.6 %collective-permute-start.92 = (bf16[4,192,384]{2,1,0:T(8,128)(2,1)}, bf16[4,192,384]{2,1,0:T(8,128)(2,1)}, u32[]{:S(2)}, u32[]{:S(2)}) collective-permute-start(bf16[4,192,384]{2,1,0:T(8,128)(2,1)} %get-tuple-element.116), channel_id=1, source_target_pairs={{0,96},{32,64},{64,32},{96,0},{1,97},{33,65},{65,33},{97,1},{2,98}... | collective-permute-start | bytes 1769480 | tf_op jit(solution)/shard_map/ppermute | solution.py:34
  354.2 36.1 %collective-permute-start.91 = (bf16[4,192,384]{2,1,0:T(8,128)(2,1)}, bf16[4,192,384]{2,1,0:T(8,128)(2,1)}, u32[]{:S(2)}, u32[]{:S(2)}) collective-permute-start(bf16[4,192,384]{2,1,0:T(8,128)(2,1)} %get-tuple-element.117), channel_id=1, source_target_pairs={{0,64},{32,96},{64,0},{96,32},{1,65},{33,97},{65,1},{97,33},{2,66}... | collective-permute-start | bytes 1769480 | tf_op jit(solution)/shard_map/ppermute | solution.py:34
  354.3 36.1 %collective-permute-start.90 = (bf16[4,192,384]{2,1,0:T(8,128)(2,1)}, bf16[4,192,384]{2,1,0:T(8,128)(2,1)}, u32[]{:S(2)}, u32[]{:S(2)}) collective-permute-start(bf16[4,192,384]{2,1,0:T(8,128)(2,1)} %get-tuple-element.115), channel_id=1, source_target_pairs={{0,32},{32,0},{64,96},{96,64},{1,33},{33,1},{65,97},{97,65},{2,34}... | collective-permute-start | bytes 1769480 | tf_op jit(solution)/shard_map/ppermute | solution.py:34
  359.9 34.8 %collective-permute-start.98 = (bf16[4,192,384]{2,1,0:T(8,128)(2,1)}, bf16[4,192,384]{2,1,0:T(8,128)(2,1)}, u32[]{:S(2)}, u32[]{:S(2)}) collective-permute-start(bf16[4,192,384]{2,1,0:T(8,128)(2,1)} %get-tuple-element.114), channel_id=1, source_target_pairs={{0,24},{8,16},{16,8},{24,0},{1,25},{9,17},{17,9},{25,1},{2,26},{10... | collective-permute-start | bytes 1769480 | tf_op jit(solution)/shard_map/ppermute | solution.py:34
  363.3 33.3 %collective-permute-start.97 = (bf16[4,192,384]{2,1,0:T(8,128)(2,1)}, bf16[4,192,384]{2,1,0:T(8,128)(2,1)}, u32[]{:S(2)}, u32[]{:S(2)}) collective-permute-start(bf16[4,192,384]{2,1,0:T(8,128)(2,1)} %get-tuple-element.113), channel_id=1, source_target_pairs={{0,16},{8,24},{16,0},{24,8},{1,17},{9,25},{17,1},{25,9},{2,18},{10... | collective-permute-start | bytes 1769480 | tf_op jit(solution)/shard_map/ppermute | solution.py:34
  410.5 33.6 %collective-permute-start.102 = (bf16[192,384]{1,0:T(8,128)(2,1)}, bf16[192,384]{1,0:T(8,128)(2,1)}, u32[]{:S(2)}, u32[]{:S(2)}) collective-permute-start(bf16[192,384]{1,0:T(8,128)(2,1)} %get-tuple-element.70), channel_id=1, source_target_pairs={{0,4},{4,0},{1,5},{5,1},{2,6},{6,2},{3,7},{7,3},{8,12},{12,8},{9,1... | collective-permute-start | bytes 442376 | tf_op jit(solution)/shard_map/ppermute | solution.py:34
  421.3 42.8 %collective-permute-start.49 = (bf16[384,512]{1,0:T(8,128)(2,1)S(1)}, bf16[384,512]{1,0:T(8,128)(2,1)}, u32[]{:S(2)}, u32[]{:S(2)}) collective-permute-start(bf16[384,512]{1,0:T(8,128)(2,1)S(1)} %get-tuple-element.19), channel_id=1, source_target_pairs={{0,2},{2,0},{1,3},{3,1},{4,6},{6,4},{5,7},{7,5},{8,10},{10,8},{9,1... | collective-permute-start | bytes 1179656 | tf_op jit(solution)/shard_map/ppermute | solution.py:34
  442.5 70.5 %collective-permute-start.61 = (bf16[384,768]{1,0:T(8,128)(2,1)}, bf16[384,768]{1,0:T(8,128)(2,1)}, u32[]{:S(2)}, u32[]{:S(2)}) collective-permute-start(bf16[384,768]{1,0:T(8,128)(2,1)} %convolution_convert_fusion.5), channel_id=1, source_target_pairs={{0,2},{2,0},{1,3},{3,1},{4,6},{6,4},{5,7},{7,5},{8,10},{10,8},{9,1... | collective-permute-start | bytes 1769480 | tf_op jit(solution)/shard_map/ppermute | solution.py:34
  462.6 55.5 %collective-permute-start.112 = (bf16[4,192,384]{2,1,0:T(8,128)(2,1)}, bf16[4,192,384]{2,1,0:T(8,128)(2,1)}, u32[]{:S(2)}, u32[]{:S(2)}) collective-permute-start(bf16[4,192,384]{2,1,0:T(8,128)(2,1)} %bitcast_dynamic-update-slice_fusion.39), channel_id=1, source_target_pairs={{0,32},{32,0},{64,96},{96,64},{1,33},{33,1},{65,97},{97,65},{2,34}... | collective-permute-start | bytes 1769480 | tf_op jit(solution)/shard_map/ppermute | solution.py:34
  495.9 70.9 %all-to-all-start.7 = ((bf16[4,256,768]{2,1,0:T(8,128)(2,1)}), bf16[4,256,768]{2,1,0:T(8,128)(2,1)}, u32[]{:S(2)}, u32[]{:S(2)}) async-start(bf16[4,256,768]{2,1,0:T(8,128)(2,1)} %bitcast.612), calls=%async_computation.7 | async-start | bytes 3145728 | tf_op jit(solution)/shard_map/all_to_all | solution.py:83
  522.2 34.7 %collective-permute-start.60 = (bf16[768,768]{1,0:T(8,128)(2,1)}, bf16[768,768]{1,0:T(8,128)(2,1)}, u32[]{:S(2)}, u32[]{:S(2)}) collective-permute-start(bf16[768,768]{1,0:T(8,128)(2,1)} %convolution_convert_fusion.4), channel_id=1, source_target_pairs={{0,2},{2,0},{1,3},{3,1},{4,6},{6,4},{5,7},{7,5},{8,10},{10,8},{9,1... | collective-permute-start | bytes 3538952 | tf_op jit(solution)/shard_map/ppermute | solution.py:34
  (211 other events, 1888.5 us)

commit v2 on v1

v2 whole, which is shorter than its diff:
```python
import jax
import jax.numpy as jnp
from jax import lax
from jax.experimental import pallas as pl
from jax.experimental.pallas import tpu as pltpu
from jax.sharding import Mesh
from jax.sharding import PartitionSpec as P

D = 1536
HD = 96
HALF = HD // 2
EPS = 1e-05
THETA = 100000.0
NEGATIVE = -1e30
SCALE = HD**-0.5
LOG2E = 1.4426950408889634
F32 = jnp.float32
BF16 = jnp.bfloat16
QUARTER = 256
TOKENS = 2 * QUARTER
CHUNK = 128
WIDE = D // 2
SHARD = D // 4
YS = ("yhi", "ylo")
DP = ("x", "z")

NN = ((1,), (0,))
NT = ((1,), (1,))
TN = ((0,), (0,))


def dot(a, b, dims):
    return lax.dot_general(a, b, (dims, ((), ())), preferred_element_type=F32)


def swap(value, axis, step=1):
    count = lax.axis_size(axis)
    return lax.ppermute(value, axis, [(i, i ^ step) for i in range(count)])


def swap_y(value, k):
    return swap(value, ("ylo", "yhi"), 2 * (k & 1) + (k >> 1))


def peers_y(value):
    return [value] + [swap_y(value, k) for k in (1, 2, 3)]


def to_peers_y(values):
    return [values[0]] + [swap_y(values[k], k) for k in (1, 2, 3)]


def gather_dp(value):
    return lax.all_gather(value, DP, axis=0)


def scatter_dp(value):
    got = lax.all_to_all(value, DP, 0, 0, tiled=True)
    return got.astype(F32).sum(axis=0).astype(BF16)


def gather_dp_now(value):
    count = lax.axis_size(DP)
    return lax.all_to_all(jnp.broadcast_to(value[None], (count, *value.shape)), DP, 0, 0, tiled=True)


def gather_y_now(value):
    return lax.all_to_all(jnp.broadcast_to(value[None], (4, *value.shape)), YS, 0, 0, tiled=True)


def small_sum(value):
    for axis in ("core", "ylo", "yhi", "x", "z"):
        parts = [value] + [swap(value, axis, k) for k in range(1, lax.axis_size(axis))]
        value = sum(parts[1:], parts[0])
    return value


def vmem():
    return pl.BlockSpec(memory_space=pltpu.VMEM)


def smem():
    return pl.BlockSpec(memory_space=pltpu.SMEM)


def shape(dims, dtype):
    return jax.ShapeDtypeStruct(dims, dtype)


def cost(flops, nbytes):
    return pl.CostEstimate(flops=int(flops), bytes_accessed=int(nbytes), transcendentals=0)


def params(mib):
    return pltpu.CompilerParams(vmem_limit_bytes=mib << 20)


def peer(spot, k):
    high = jnp.bitwise_xor(spot[0], k >> 1)
    low = jnp.bitwise_xor(spot[1], k & 1)
    return high, low, 2 * high + low


def place_pieces(spot, pieces, out):
    for k, piece in enumerate(pieces):
        high, low, _ = peer(spot, k)
        rows = pl.ds(pl.multiple_of(high * QUARTER, QUARTER), QUARTER)
        for j in range(2):
            lanes = pl.ds(pl.multiple_of(low * SHARD + j * WIDE, 128), SHARD)
            out[rows, lanes] = piece[j]


def cut_pieces(spot, value, outs):
    for k, out in enumerate(outs):
        high, low, _ = peer(spot, k)
        rows = pl.ds(pl.multiple_of(high * QUARTER, QUARTER), QUARTER)
        for j in range(2):
            lanes = pl.ds(pl.multiple_of(low * SHARD + j * WIDE, 128), SHARD)
            out[j] = value[rows, lanes].astype(out.dtype)


def turn(front, behind, cosine, sine):
    return front * cosine - behind * sine, behind * cosine + front * sine


def qkv_kernel(spot, p0, p1, p2, p3, gain, own, oth, cosine, sine, x, h, inv, q, kv):
    place_pieces(spot, (p0, p1, p2, p3), x)
    for i in range(4):
        rows = pl.ds(i * CHUNK, CHUNK)
        value = x[rows].astype(F32)
        inverse = lax.rsqrt((value * value).sum(axis=-1, keepdims=True) / D + EPS)
        inv[rows] = inverse
        h[rows] = (value * inverse * gain[...]).astype(BF16)
    cos, sin = cosine[...], sine[...]
    for i in range(4):
        rows = pl.ds(i * 2 * HD, 2 * HD)
        raw = dot(own[rows], h[:, :WIDE], NT) + dot(oth[rows], h[:, WIDE:], NT)
        out, base = (q, i * 2 * HD) if i < 2 else (kv, (i - 2) * 2 * HD)
        for head in range(2):
            front, behind = raw[head * HD : head * HD + HALF], raw[head * HD + HALF : (head + 1) * HD]
            if i < 2 or head == 0:
                front, behind = turn(front, behind, cos, sin)
            out[pl.ds(base + head * HD, HALF)] = front.astype(BF16)
            out[pl.ds(base + head * HD + HALF, HALF)] = behind.astype(BF16)


def project(spot, pieces, gain, own, oth, cosine, sine):
    return pl.pallas_call(
        qkv_kernel,
        out_shape=(
            shape((TOKENS, D), BF16),
            shape((TOKENS, D), BF16),
            shape((TOKENS, 1), F32),
            shape((SHARD, TOKENS), BF16),
            shape((SHARD, TOKENS), BF16),
        ),
        in_specs=[smem()] + [vmem()] * 9,
        out_specs=(vmem(),) * 5,
        compiler_params=params(32),
        cost_estimate=cost(2 * TOKENS * D * WIDE, 8 << 20),
        name="project",
    )(spot, *pieces, gain, own, oth, cosine, sine)


def key_blocks(block):
    return (0, 2) if block == 0 else (0, 1, 2, 3)


def allowed_keys(spot, key, place, low):
    at = spot[4 + key] + lax.broadcasted_iota(jnp.int32, (QUARTER, place.shape[1]), 0)
    return (at >= low) & (at <= place)


def two_heads(ref, group, block):
    lanes = pl.ds(block * QUARTER, QUARTER)
    return jnp.concatenate(
        [ref[pl.ds((2 * group + h) * HD, HD), lanes] for h in range(2)], axis=1
    )


def twice(ref, block):
    row = ref[:, pl.ds(block * QUARTER, QUARTER)]
    return jnp.concatenate([row, row], axis=1)


def forward_kernel(spot, q_ref, own_ref, oth_ref, place_ref, low_ref, outt_ref, out_ref, lse_ref):
    factor = SCALE * LOG2E
    for group in range(2):
        keys = []
        vals = []
        for ref in (own_ref, oth_ref):
            for half in range(2):
                lanes = pl.ds(half * QUARTER, QUARTER)
                keys.append(ref[pl.ds(group * 2 * HD, HD), lanes].T)
                vals.append(ref[pl.ds(group * 2 * HD + HD, HD), lanes])
        for block in range(2):
            q = two_heads(q_ref, group, block)
            place, low = twice(place_ref, block), twice(low_ref, block)
            scores = []
            for key in key_blocks(block):
                s = dot(keys[key], q, NN)
                scores.append(jnp.where(allowed_keys(spot, key, place, low), s, NEGATIVE))
            peak = scores[0].max(axis=0, keepdims=True)
            for s in scores[1:]:
                peak = jnp.maximum(peak, s.max(axis=0, keepdims=True))
            shift = peak * factor
            total = jnp.zeros_like(peak)
            acc = jnp.zeros((HD, 2 * QUARTER), F32)
            for key, s in zip(key_blocks(block), scores):
                p = jnp.exp2(s * factor - shift)
                total = total + p.sum(axis=0, keepdims=True)
                acc = acc + dot(vals[key], p.astype(BF16), NN)
            acc = (acc / total).astype(BF16)
            lse = shift + jnp.log2(total)
            for h in range(2):
                lanes = pl.ds(block * QUARTER, QUARTER)
                cut = slice(h * QUARTER, (h + 1) * QUARTER)
                outt_ref[pl.ds((2 * group + h) * HD, HD), lanes] = acc[:, cut]
                lse_ref[pl.ds(2 * group + h, 1), lanes] = lse[:, cut]
    out_ref[...] = outt_ref[...].T


def attend(spot, queries, own, other, place, low):
    return pl.pallas_call(
        forward_kernel,
        out_shape=(
            shape((SHARD, TOKENS), BF16),
            shape((TOKENS, SHARD), BF16),
            shape((4, TOKENS), F32),
        ),
        in_specs=[smem()] + [vmem()] * 5,
        out_specs=(vmem(),) * 3,
        compiler_params=params(40),
        cost_estimate=cost(4 * 4 * HD * QUARTER * QUARTER * 6, 4 << 20),
        name="attend_forward",
    )(spot, queries, own, other, place, low)


def mix_kernel(spot, x, h0, h1, h2, h3, own, oth, gain, mixed, h, inv, heads):
    for k, piece in enumerate((h0, h1, h2, h3)):
        _, _, y = peer(spot, k)
        heads[:, pl.ds(pl.multiple_of(y * SHARD, 128), SHARD)] = piece[...]
    for i in range(2):
        rows = pl.ds(i * QUARTER, QUARTER)
        square = jnp.zeros((QUARTER, 1), F32)
        for j, w in enumerate((own, oth)):
            lanes = pl.ds(j * WIDE, WIDE)
            value = x[rows, lanes].astype(F32)
            for half in range(2):
                block = w[:, half].reshape(WIDE, WIDE)
                value = value + dot(heads[rows, pl.ds(half * WIDE, WIDE)], block, NN)
            mixed[rows, lanes] = value
            square = square + (value * value).sum(axis=-1, keepdims=True)
        inverse = lax.rsqrt(square / D + EPS)
        inv[rows] = inverse
        h[rows] = (mixed[rows] * inverse * gain[...]).astype(BF16)


def mix(spot, x, pieces, own, oth, gain):
    return pl.pallas_call(
        mix_kernel,
        out_shape=(
            shape((TOKENS, D), F32),
            shape((TOKENS, D), BF16),
            shape((TOKENS, 1), F32),
        ),
        in_specs=[smem()] + [vmem()] * 8,
        out_specs=(vmem(),) * 3,
        scratch_shapes=[pltpu.VMEM((TOKENS, D), BF16)],
        compiler_params=params(40),
        cost_estimate=cost(2 * TOKENS * D * D, 12 << 20),
        name="mix",
    )(spot, x, *pieces, own, oth, gain)


def units_of(ref, k):
    return ref[:, k].reshape(-1, WIDE)


def feed_kernel(spot, h, g0, g1, g2, g3, own, oth, top, act, dgate, dup, o0, o1, o2, o3, acc):
    step = pl.program_id(0)

    @pl.when(step == 0)
    def _():
        place_pieces(spot, (g0, g1, g2, g3), top)
        acc[...] = jnp.zeros_like(acc)

    def hidden(k, columns):
        return dot(units_of(own, k), columns[:, :WIDE], NT) + dot(
            units_of(oth, k), columns[:, WIDE:], NT
        )

    gate, up, grad = hidden(0, h), hidden(1, h), hidden(2, top)
    sigma = jax.nn.sigmoid(gate)
    silu = gate * sigma
    act[...] = (silu * up).astype(BF16)
    grad_gate = (grad * up * sigma * (1.0 + gate * (1.0 - sigma))).astype(BF16)
    grad_up = (grad * silu).astype(BF16)
    dgate[...] = grad_gate
    dup[...] = grad_up
    grad_gate, grad_up = grad_gate.T, grad_up.T
    for j, w in enumerate((own, oth)):
        lanes = pl.ds(j * WIDE, WIDE)
        acc[:, lanes] += dot(grad_gate, units_of(w, 0), NN) + dot(grad_up, units_of(w, 1), NN)

    @pl.when(step == pl.num_programs(0) - 1)
    def _():
        for k, out in enumerate((o0, o1, o2, o3)):
            _, _, y = peer(spot, k)
            out[...] = acc[pl.ds(pl.multiple_of(y * CHUNK, CHUNK), CHUNK)].astype(BF16)


def whole(dims):
    return pl.BlockSpec(dims, lambda *_: (0,) * len(dims))


def feed(spot, h, pieces, own, oth):
    steps = 4
    units = own.shape[0] * own.shape[2]
    group = own.shape[0] // steps
    rows = units // steps
    weights = pl.BlockSpec((group, *own.shape[1:]), lambda i, _: (i, 0, 0, 0))
    block = pl.BlockSpec((rows, TOKENS), lambda i, _: (i, 0))
    return pl.pallas_call(
        feed_kernel,
        out_shape=(
            shape((TOKENS, D), BF16),
            *(shape((units, TOKENS), BF16),) * 3,
            *(shape((CHUNK, D), BF16),) * 4,
        ),
        grid_spec=pltpu.PrefetchScalarGridSpec(
            num_scalar_prefetch=1,
            grid=(steps,),
            in_specs=[whole((TOKENS, D))]
            + [whole((2, QUARTER, SHARD))] * 4
            + [weights, weights],
            out_specs=(whole((TOKENS, D)), block, block, block, *(whole((CHUNK, D)),) * 4),
            scratch_shapes=[pltpu.VMEM((TOKENS, D), F32)],
        ),
        compiler_params=params(48),
        cost_estimate=cost(10 * TOKENS * D * units, 20 << 20),
        name="feed",
    )(spot, h, *pieces, own, oth)


def down_kernel(spot, act, own, oth, o0, o1, o2, o3, acc):
    step = pl.program_id(0)

    @pl.when(step == 0)
    def _():
        acc[...] = jnp.zeros_like(acc)

    hidden = act[...].T
    for j, w in enumerate((own, oth)):
        acc[:, pl.ds(j * WIDE, WIDE)] += dot(hidden, w[...].reshape(-1, WIDE), NN)

    @pl.when(step == pl.num_programs(0) - 1)
    def _():
        cut_pieces(spot, acc, (o0, o1, o2, o3))


def down(spot, act, own, oth):
    steps = 4
    group = own.shape[0] // steps
    rows = act.shape[0] // steps
    weights = pl.BlockSpec((group, 1, *own.shape[2:]), lambda i, _: (i, 2, 0, 0))
    return pl.pallas_call(
        down_kernel,
        out_shape=(shape((2, QUARTER, SHARD), BF16),) * 4,
        grid_spec=pltpu.PrefetchScalarGridSpec(
            num_scalar_prefetch=1,
            grid=(steps,),
            in_specs=[pl.BlockSpec((rows, TOKENS), lambda i, _: (i, 0)), weights, weights],
            out_specs=(whole((2, QUARTER, SHARD)),) * 4,
            scratch_shapes=[pltpu.VMEM((TOKENS, D), F32)],
        ),
        compiler_params=params(24),
        cost_estimate=cost(2 * TOKENS * D * act.shape[0], 8 << 20),
        name="down",
    )(spot, act, own, oth)


def residual_kernel(spot, r0, r1, r2, r3, mixed, inv, top, gain, out, part):
    grad = r0[...].astype(F32) + r1[...].astype(F32) + r2[...].astype(F32) + r3[...].astype(F32)
    inverse = inv[...]
    normed = mixed[...] * inverse
    part[...] = (grad * normed).sum(axis=0, keepdims=True)
    scaled = grad * gain[...]
    inner = (scaled * normed).sum(axis=-1, keepdims=True) / D
    out[...] = (top[...].astype(F32) + inverse * (scaled - normed * inner)).astype(BF16)


def residual(spot, pieces, mixed, inv, top, gain):
    mine = lambda width: pl.BlockSpec((CHUNK, width), lambda i, s: (2 * s[0] + s[1], 0))
    return pl.pallas_call(
        residual_kernel,
        out_shape=(shape((CHUNK, D), BF16), shape((1, D), F32)),
        grid_spec=pltpu.PrefetchScalarGridSpec(
            num_scalar_prefetch=1,
            grid=(1,),
            in_specs=[whole((CHUNK, D))] * 4 + [mine(D), mine(1), mine(D), whole((1, D))],
            out_specs=(whole((CHUNK, D)), whole((1, D))),
        ),
        compiler_params=params(16),
        cost_estimate=cost(CHUNK * D * 20, 4 << 20),
        name="residual",
    )(spot, *pieces, mixed, inv, top, gain)


def backward_kernel(
    spot, r0, r1, r2, r3, wown, woth, q_ref, own_ref, oth_ref, o_ref, lse_ref, place_ref, low_ref,
    cosine, sine, rows_ref, dq_ref, down_ref, doth_ref, do_ref,
):
    for k, piece in enumerate((r0, r1, r2, r3)):
        _, _, y = peer(spot, k)
        rows_ref[pl.ds(pl.multiple_of(y * CHUNK, CHUNK), CHUNK)] = piece[...]
    do_ref[...] = (
        dot(wown[...].reshape(SHARD, WIDE), rows_ref[:, :WIDE], NT)
        + dot(woth[...].reshape(SHARD, WIDE), rows_ref[:, WIDE:], NT)
    ).astype(BF16)
    factor = SCALE * LOG2E
    for group in range(2):
        keys, vals, keyst = [], [], []
        for ref in (own_ref, oth_ref):
            for half in range(2):
                lanes = pl.ds(half * QUARTER, QUARTER)
                kt = ref[pl.ds(group * 2 * HD, HD), lanes]
                keyst.append(kt)
                keys.append(kt.T)
                vals.append(ref[pl.ds(group * 2 * HD + HD, HD), lanes].T)
        dks = [jnp.zeros((HD, QUARTER), F32) for _ in range(4)]
        dvs = [jnp.zeros((HD, QUARTER), F32) for _ in range(4)]
        for block in range(2):
            lanes = pl.ds(block * QUARTER, QUARTER)
            q = two_heads(q_ref, group, block)
            do = two_heads(do_ref, group, block)
            o = two_heads(o_ref, group, block)
            place, low = twice(place_ref, block), twice(low_ref, block)
            lse = jnp.concatenate(
                [lse_ref[pl.ds(2 * group + h, 1), lanes] for h in range(2)], axis=1
            )
            delta = (do.astype(F32) * o.astype(F32)).sum(axis=0, keepdims=True)
            dq = jnp.zeros((HD, 2 * QUARTER), F32)
            for key in key_blocks(block):
                s = dot(keys[key], q, NN)
                p = jnp.exp2(s * factor - lse)
                p = jnp.where(allowed_keys(spot, key, place, low), p, 0.0)
                dp = dot(vals[key], do, NN)
                ds = (p * (dp - delta)).astype(BF16)
                dvs[key] = dvs[key] + dot(do, p.astype(BF16), NT)
                dks[key] = dks[key] + dot(q, ds, NT)
                dq = dq + dot(keyst[key], ds, NN)
            dq = dq * SCALE
            cos, sin = twice(cosine, block), twice(sine, block)
            front, behind = turn(dq[:HALF], dq[HALF:], cos, -sin)
            for h in range(2):
                cut = slice(h * QUARTER, (h + 1) * QUARTER)
                base = (2 * group + h) * HD
                dq_ref[pl.ds(base, HALF), lanes] = front[:, cut].astype(BF16)
                dq_ref[pl.ds(base + HALF, HALF), lanes] = behind[:, cut].astype(BF16)
        for i, ref in enumerate((down_ref, doth_ref)):
            for half in range(2):
                lanes = pl.ds(half * QUARTER, QUARTER)
                rows = group * 2 * HD
                ref[pl.ds(rows, HD), lanes] = (dks[2 * i + half] * SCALE).astype(ref.dtype)
                ref[pl.ds(rows + HD, HD), lanes] = dvs[2 * i + half].astype(ref.dtype)


def attend_back(spot, pieces, wown, woth, queries, own, other, outs, lse, place, low, cosine, sine):
    half = wown.shape[0] // 2
    weights = pl.BlockSpec((half, 1, *wown.shape[2:]), lambda i, s: (s[1], s[0], 0, 0))
    flat = whole((SHARD, TOKENS))
    row = whole((1, TOKENS))
    return pl.pallas_call(
        backward_kernel,
        out_shape=(
            shape((TOKENS, D), BF16),
            shape((SHARD, TOKENS), BF16),
            shape((SHARD, TOKENS), F32),
            shape((SHARD, TOKENS), BF16),
        ),
        grid_spec=pltpu.PrefetchScalarGridSpec(
            num_scalar_prefetch=1,
            grid=(1,),
            in_specs=[whole((CHUNK, D))] * 4
            + [weights, weights, flat, flat, flat, flat, whole((4, TOKENS)), row, row]
            + [whole((HALF, TOKENS))] * 2,
            out_specs=(whole((TOKENS, D)), flat, flat, flat),
            scratch_shapes=[pltpu.VMEM((SHARD, TOKENS), BF16)],
        ),
        compiler_params=params(48),
        cost_estimate=cost(10 * 4 * HD * QUARTER * QUARTER * 6 + 2 * TOKENS * D * SHARD, 8 << 20),
        name="attend_backward",
    )(spot, *pieces, wown, woth, queries, own, other, outs, lse, place, low, cosine, sine)


def input_kernel(
    spot, dq, mine, got, cosine, sine, own, oth, x, inv, raw, o0, o1, o2, o3, part, acc
):
    raw[:SHARD] = dq[...]
    total = mine[...] + got[...].astype(F32)
    cos, sin = cosine[...], -sine[...]
    for group in range(2):
        base = group * 2 * HD
        front, behind = turn(total[base : base + HALF], total[base + HALF : base + HD], cos, sin)
        raw[pl.ds(SHARD + base, HALF)] = front.astype(BF16)
        raw[pl.ds(SHARD + base + HALF, HALF)] = behind.astype(BF16)
        raw[pl.ds(SHARD + base + HD, HD)] = total[base + HD : base + 2 * HD].astype(BF16)
    grads = raw[...].T
    for j, w in enumerate((own, oth)):
        lanes = pl.ds(j * WIDE, WIDE)
        value = dot(grads, w[...], NN)
        acc[:, lanes] = value.astype(BF16)
        part[:, lanes] = (value * (x[:, lanes].astype(F32) * inv[...])).sum(axis=0, keepdims=True)
    cut_pieces(spot, acc, (o0, o1, o2, o3))


def input_grad(spot, dq, mine, got, cosine, sine, own, oth, x, inv):
    return pl.pallas_call(
        input_kernel,
        out_shape=(
            shape((WIDE, TOKENS), BF16),
            *(shape((2, QUARTER, SHARD), BF16),) * 4,
            shape((1, D), F32),
        ),
        in_specs=[smem()] + [vmem()] * 9,
        out_specs=(vmem(),) * 6,
        scratch_shapes=[pltpu.VMEM((TOKENS, D), BF16)],
        compiler_params=params(32),
        cost_estimate=cost(2 * TOKENS * D * WIDE, 8 << 20),
        name="input_grad",
    )(spot, dq, mine, got, cosine, sine, own, oth, x, inv)


def units_grad_kernel(dgate, dup, act, h, top, *rest):
    out = rest[-1]
    for k, (rows, columns) in enumerate(((dgate, h), (dup, h), (act, top))):
        value = dot(rows[...], columns[...], NN).reshape(out.shape[0], -1, WIDE)
        if len(rest) == 2:
            value = value + rest[0][:, k].astype(F32)
        out[:, k] = value.astype(BF16)


def units_grad(dgate, dup, act, h, top, half, got, ndp):
    steps = 4
    units = dgate.shape[0]
    block = pl.BlockSpec((units // steps, TOKENS), lambda i: (i, 0))
    columns = pl.BlockSpec((TOKENS, WIDE), lambda i: (0, half))
    dims = (ndp, 3, units // ndp, WIDE)
    result = pl.BlockSpec((ndp // steps, *dims[1:]), lambda i: (i, 0, 0, 0))
    extra = [] if got is None else [got]
    return pl.pallas_call(
        units_grad_kernel,
        grid=(steps,),
        out_shape=shape(dims, BF16),
        in_specs=[block, block, block, columns, columns] + [result] * len(extra),
        out_specs=result,
        compiler_params=params(32),
        cost_estimate=cost(6 * TOKENS * WIDE * units, 12 << 20),
        name="units_grad",
    )(dgate, dup, act, h, top, *extra)


def heads_grad_kernel(raw, heads, h, rows, *rest):
    out = rest[-1]
    for i, (left, right) in enumerate(((raw[:SHARD], h), (raw[SHARD:], h), (heads[...], rows))):
        value = dot(left, right[...], NN)
        cut = pl.ds(i * SHARD, SHARD)
        if len(rest) == 2:
            value = value + rest[0][cut].astype(F32)
        out[cut] = value.astype(BF16)


def heads_grad(raw, heads, h, rows, half, got):
    columns = pl.BlockSpec((TOKENS, WIDE), lambda i: (0, half))
    extra = [] if got is None else [got]
    result = whole((3 * SHARD, WIDE))
    return pl.pallas_call(
        heads_grad_kernel,
        grid=(1,),
        out_shape=shape((3 * SHARD, WIDE), BF16),
        in_specs=[whole((WIDE, TOKENS)), whole((SHARD, TOKENS)), columns, columns]
        + [result] * len(extra),
        out_specs=result,
        compiler_params=params(24),
        cost_estimate=cost(6 * TOKENS * WIDE * SHARD, 6 << 20),
        name="heads_grad",
    )(raw, heads, h, rows, *extra)


def finish_units_kernel(value, gate, up, lower):
    for k, out in enumerate((gate, up)):
        out[...] = value[0, :, k].reshape(-1, SHARD).astype(F32).T
    lower[...] = value[0, :, 2].reshape(-1, SHARD).astype(F32)


def finish_units(value):
    ndp, _, _, units, _ = value.shape
    total = 2 * units * ndp
    across = pl.BlockSpec((SHARD, 2 * units), lambda i: (0, i))
    return pl.pallas_call(
        finish_units_kernel,
        grid=(ndp,),
        out_shape=(shape((SHARD, total), F32),) * 2 + (shape((total, SHARD), F32),),
        in_specs=[pl.BlockSpec((1, *value.shape[1:]), lambda i: (i, 0, 0, 0, 0))],
        out_specs=(across, across, pl.BlockSpec((2 * units, SHARD), lambda i: (i, 0))),
        compiler_params=params(16),
        cost_estimate=cost(0, 14 << 20),
        name="finish_units",
    )(value)


def body(tokens, gain1, w_query, w_keyval, w_out, gain2, w_gate, w_up, w_down, grad_out, segments):
    core, yh, yl = lax.axis_index("core"), lax.axis_index("yhi"), lax.axis_index("ylo")
    ndp = lax.axis_size(DP)
    dp = lax.axis_index(DP)
    mine = core ^ yh
    spot = jnp.stack(
        [yh, yl, 2 * yh + yl, core]
        + [place * QUARTER for place in (core, 3 - core, 1 - core, 2 + core)]
    ).astype(jnp.int32)

    def pick(first_is_mine, own, other):
        return jnp.where(first_is_mine, own, other), jnp.where(first_is_mine, other, own)

    def whole_rows(value):
        own = lax.dynamic_slice_in_dim(value, mine * QUARTER, QUARTER, 0)
        other = lax.dynamic_slice_in_dim(value, (1 - mine) * QUARTER, QUARTER, 0)
        return peers_y(jnp.stack([own, swap(other, "core")]))

    x_pieces = whole_rows(tokens[0])

    gains = jnp.stack([gain1, gain2])
    gains = jnp.stack([gains, swap(gains, "core")], axis=1)
    gains = jnp.stack(pick(yl == 0, gains, swap(gains, "ylo")), axis=2).reshape(2, 1, D)

    def part_of(value, dim):
        size = value.shape[dim] // ndp
        return lax.dynamic_slice_in_dim(value, dp * size, size, dim)

    def exchanged(slab):
        send = lax.dynamic_index_in_dim(slab, 1 - yl, 0, keepdims=False)
        keep = lax.dynamic_index_in_dim(slab, yl, 0, keepdims=False)
        return jnp.concatenate(pick(yl == 0, keep, swap(send, "ylo")), axis=-1)

    def rows_first(weight):
        return weight.T.reshape(2, -1, SHARD)

    qkv_own = exchanged(jnp.concatenate([rows_first(w_query), rows_first(w_keyval)], axis=1))
    qkv_oth = swap(qkv_own, "core")

    piece = gather_y_now(part_of(w_out, 0)).reshape(2, 2, -1, SHARD)
    piece = piece.transpose(0, 2, 1, 3).reshape(2, -1, WIDE)
    out_own = gather_dp_now(piece)
    out_oth = swap(out_own, "core")

    slabs = [part_of(w_gate, 1).T, part_of(w_up, 1).T, part_of(w_down, 0)]
    slab = jnp.stack([s.reshape(2, -1, SHARD) for s in slabs], axis=1)
    feed_own = gather_dp(exchanged(slab))
    feed_oth = swap(feed_own, "core")

    ids = segments[0]
    low_all = jnp.sum((ids[None, :] < ids[:, None]).astype(jnp.int32), axis=1)
    low = jnp.concatenate(
        [
            lax.dynamic_slice_in_dim(low_all, core * QUARTER, QUARTER),
            lax.dynamic_slice_in_dim(low_all, (3 - core) * QUARTER, QUARTER),
        ]
    )
    step = jnp.arange(QUARTER, dtype=jnp.int32)
    place = jnp.concatenate([core * QUARTER + step, (3 - core) * QUARTER + step])
    rates = THETA ** (-jnp.arange(HALF, dtype=F32) * 2.0 / HD)
    angles = rates[:, None] * (place - low).astype(F32)[None, :]
    cosine, sine = jnp.cos(angles), jnp.sin(angles)
    place, low = place[None, :], low[None, :]

    x, h_one, inv_one, queries, keyval = project(
        spot, x_pieces, gains[0], qkv_own, qkv_oth, cosine, sine
    )
    keyval_oth = swap(keyval, "core")
    heads_t, heads, lse = attend(spot, queries, keyval, keyval_oth, place, low)
    mixed, h_two, inv_two = mix(spot, x, peers_y(heads), out_own, out_oth, gains[1])

    top_pieces = whole_rows(grad_out[0])
    top, act, dgate, dup, *parts = feed(spot, h_two, top_pieces, feed_own, feed_oth)
    rows, gain2_part = residual(spot, to_peers_y(parts), mixed, inv_two, top, gains[1])

    row_all, dq, dkv, dkv_oth = attend_back(
        spot, peers_y(rows), out_own, out_oth, queries, keyval, keyval_oth, heads_t, lse, place, low,
        cosine, sine,
    )
    raw, *parts, gain1_part = input_grad(
        spot, dq, dkv, swap(dkv_oth, "core"), cosine, sine, qkv_own, qkv_oth, x, inv_one
    )
    got = sum([g.astype(F32) for g in to_peers_y(parts)])

    def my_block(value):
        return jnp.stack(
            [
                lax.dynamic_slice(value, (yh * QUARTER, j * WIDE + yl * SHARD), (QUARTER, SHARD))
                for j in range(2)
            ]
        )

    def to_home(block):
        return jnp.concatenate(pick(mine == 0, block[0], swap(block[1], "core")))

    gain = jnp.stack(
        [lax.dynamic_slice(gains[0], (0, j * WIDE + yl * SHARD), (1, SHARD)) for j in range(2)]
    )
    inverse = lax.dynamic_slice_in_dim(inv_one, yh * QUARTER, QUARTER, 0)
    normed = my_block(x).astype(F32) * inverse
    scaled = got * gain
    inner = (scaled * normed).sum(axis=(0, 2))
    inner = (inner + swap(inner, "ylo"))[:, None] / D
    grad_in = to_home(my_block(row_all).astype(F32) + inverse * (scaled - normed * inner))

    parts = to_peers_y(down(spot, act, feed_own, feed_oth))
    output = my_block(mixed) + sum([g.astype(F32) for g in parts])
    output = to_home(output.astype(BF16))

    def exchanged_back(value):
        keep = lax.dynamic_slice_in_dim(value, yl * SHARD, SHARD, value.ndim - 1)
        send = lax.dynamic_slice_in_dim(value, (1 - yl) * SHARD, SHARD, value.ndim - 1)
        return jnp.stack(pick(yl == 0, keep, swap(send, "ylo")))

    send = units_grad(dgate, dup, act, h_two, top, 1, None, ndp)
    total = units_grad(dgate, dup, act, h_two, top, 0, swap(send, "core"), ndp)
    total = gather_dp(exchanged_back(scatter_dp(total)))
    grad_w_gate, grad_w_up, grad_w_down = finish_units(total)

    send = heads_grad(raw, heads_t, h_one, row_all, 1, None)
    total = heads_grad(raw, heads_t, h_one, row_all, 0, swap(send, "core"))
    total = exchanged_back(scatter_dp(total.reshape(ndp, -1, WIDE)))
    total = gather_dp_now(total)
    both = total.reshape(ndp, 2, -1, SHARD).transpose(1, 0, 2, 3).reshape(2, -1, SHARD).astype(F32)
    grad_w_query = both[:, :SHARD].reshape(-1, SHARD).T
    grad_w_keyval = both[:, SHARD : 2 * SHARD].reshape(-1, SHARD).T
    grad_w_out = both[:, 2 * SHARD :].reshape(-1, SHARD)

    parts = small_sum(relative_to_absolute(core, jnp.concatenate([gain1_part, gain2_part])))
    parts = lax.dynamic_slice(parts, (0, core * WIDE + yl * SHARD), (2, SHARD))
    return (
        output[None],
        grad_in[None],
        parts[0],
        grad_w_query,
        grad_w_keyval,
        grad_w_out,
        parts[1],
        grad_w_gate,
        grad_w_up,
        grad_w_down,
    )


def relative_to_absolute(core, value):
    turned = jnp.concatenate([value[:, WIDE:], value[:, :WIDE]], axis=1)
    return jnp.where(core == 0, value, turned)


def solution(mesh):
    dp = mesh.shape["dp"]
    side = int(round(dp**0.5))
    fine = Mesh(
        mesh.devices.reshape(side, dp // side, 2, 2, 2), ("x", "z", "ylo", "core", "yhi")
    )
    seq, row, col = DP, ("ylo", "core"), "yhi"
    return jax.shard_map(
        body,
        mesh=fine,
        in_specs=(
            P(seq, col, row),
            P(row),
            P(row, col),
            P(row, col),
            P(col, row),
            P(row),
            P(row, col),
            P(row, col),
            P(col, row),
            P(seq, col, row),
            P(seq, None),
        ),
        out_specs=(
            P(seq, col, row),
            P(seq, col, row),
            P(row),
            P(row, col),
            P(row, col),
            P(col, row),
            P(row),
            P(row, col),
            P(row, col),
            P(col, row),
        ),
        check_vma=False,
    )
```

time: 636 us -> 527 us (0.83)
  waiting for transfers between devices: 137 us -> 263 us
  local copies, waits for them, and re-layouts: 171 us -> 54.5 us
  starting transfers between devices: 184 us -> 89.4 us
  matrix products: 57 us -> 0 us
  Pallas kernels: 8.85 us -> 65.3 us
  other arithmetic: 63.2 us -> 19.2 us
  between operations: 3.63 us -> 15.3 us
  blocking collectives: 0 us -> 10.5 us
    ppermute x115 -> x48, starting transfers between devices: 145 us -> 54.4 us  [swap(): return lax.ppermute(value, axis, [(i, i ^ step) for i in range(count)])]
    all_to_all x9 -> x4, waiting for transfers between devices: 5.29 us -> 72.9 us  [the longest x2 72.2 us: scatter_dp(): got = lax.all_to_all(value, DP, 0, 0, tiled=True)]
    dot_general x20 -> x0, matrix products: 57 us -> none  [dot(): return lax.dot_general(a, b, (dims, ((), ())), preferred_element_type=F32)]
    pallas_call x2 -> x13, Pallas kernels: 8.85 us -> 65.3 us  [the longest x1 15.5 us: feed(): pl.pallas_call(feed_kernel, out_shape=(shape((TOKENS, D), BF16), *(shape(...]
    all_gather x0 -> x2, waiting for transfers between devices: none -> 53.5 us  [gather_dp(): return lax.all_gather(value, DP, axis=0)]
    dynamic_slice x16 -> x5, local copies, waits for them, and re-layouts: 34.5 us -> 1.15 us  [the longest x2 0.94 us: exchanged_back(): lax.dynamic_slice_in_dim(value, (1 - yl) * SHARD, SHARD, value.ndim - 1)]
    dynamic_update_slice x79 -> x0, local copies, waits for them, and re-layouts: 27.3 us -> none  [placed(): out = lax.dynamic_update_index_in_dim(out, part, me ^ k, 0)]
    reshape x9 -> x4, local copies, waits for them, and re-layouts: 24.6 us -> 3.37 us  [the longest x1 1.38 us: body(): grad_w_query = both[:, :SHARD].reshape(-1, SHARD).T]
  transfers between devices with their start and end apart: 124 -> 54, of which waited for: 45 -> 26; matrix products, arithmetic and copies ran while one was open for 38% -> 5% of each run, Pallas kernels for 1% -> 7%
where the time goes in v2:
time: 527 us; the launch traced here: 517 us
  waiting for transfers between devices  263 us (50%)
  starting transfers between devices  89.4 us (17%)
  Pallas kernels  65.3 us (12%)
  local copies, waits for them, and re-layouts  54.5 us (10%)
  other arithmetic  19.2 us (4%)
  between operations  15.3 us (3%)
  blocking collectives  10.5 us (2%)
    ppermute x48, waiting for transfers between devices, swap(): return lax.ppermute(value, axis, [(i, i ^ step) for i in range(count)])  136 us
    all_to_all x2, waiting for transfers between devices, scatter_dp(): got = lax.all_to_all(value, DP, 0, 0, tiled=True)  72.2 us
    ppermute x48, starting transfers between devices, swap(): return lax.ppermute(value, axis, [(i, i ^ step) for i in range(count)])  54.4 us
    all_gather x2, waiting for transfers between devices, gather_dp(): return lax.all_gather(value, DP, axis=0)  53.5 us
    unnamed x172, local copies, waits for them, and re-layouts  39 us
    all_to_all x2, starting transfers between devices, scatter_dp(): got = lax.all_to_all(value, DP, 0, 0, tiled=True)  18.2 us
    all_to_all x2, starting transfers between devices, gather_dp_now(): lax.all_to_all(jnp.broadcast_to(value[None], (count, *value.shape)), DP,...  16.7 us
    pallas_call x1, Pallas kernels, feed(): pl.pallas_call(feed_kernel, out_shape=(shape((TOKENS, D), BF16), *(shape(...  15.5 us
  transfers between devices with their start and end apart: 54, of which 26 were waited for; matrix products, arithmetic and copies ran while one was open for 5% of the time, Pallas kernels for 7%

profile of v2, /device:TPU:0, one launch (start us, length us, event | category | flops | bytes accessed | tf_op | source)
XLA Modules:
  0.0 517.1 jit_solution(4267092011715310325)
XLA Ops:
  17.1 10.5 %all_to_all.25 = bf16[4,48,384]{2,1,0:T(8,128)(2,1)S(1)} all-to-all(bf16[4,48,384]{2,1,0:T(8,128)(2,1)S(1)} %broadcast_in_dim.18), channel_id=1, replica_groups=mesh['x'=4,'z'=4,'ylo'=2,'core'=2,'yhi'=2] {'yhi','ylo'}, dimensions={0} | all-to-all | bytes 294912 | tf_op jit(solution)/shard_map/all_to_all | solution.py:68
  29.3 8.1 %all-to-all-start.1 = ((bf16[16,2,48,768]{3,2,1,0:T(8,128)(2,1)}), bf16[16,2,48,768]{3,2,1,0:T(8,128)(2,1)}, u32[]{:S(2)}, u32[]{:S(2)}) async-start(bf16[16,2,48,768]{3,2,1,0:T(8,128)(2,1)} %broadcast_in_dim.20), calls=%async_computation.1 | async-start | bytes 4718592 | tf_op jit(solution)/shard_map/all_to_all | solution.py:64
  37.3 53.5 %all-gather.5.cloned.1.call-done = bf16[48,64,768]{2,1,0:T(8,128)(2,1)} async-done(((bf16[3,64,768]{2,1,0:T(8,128)(2,1)}), bf16[48,64,768]{2,1,0:T(8,128)(2,1)}) %all-gather.5.cloned.1.call-update) | async-done | bytes 4718608 | tf_op jit(solution)/shard_map/all_gather | solution.py:54
  94.5 12.9 %collective-permute-done.6 = bf16[768,384]{1,0:T(8,128)(2,1)S(1)} collective-permute-done((bf16[768,384]{1,0:T(8,128)(2,1)S(1)}, bf16[768,384]{1,0:T(8,128)(2,1)S(1)}, u32[]{:S(2)}, u32[]{:S(2)}) %collective-permute-start.6) | collective-permute-done | bytes 589856 | tf_op jit(solution)/shard_map/ppermute | solution.py:38
  110.8 9.0 %collective-permute-done.5 = f32[2,2,384]{2,1,0:T(2,128)S(1)} collective-permute-done((f32[2,2,384]{2,1,0:T(2,128)S(1)}, f32[2,2,384]{2,1,0:T(2,128)S(1)}, u32[]{:S(2)}, u32[]{:S(2)}) %collective-permute-start.5) | collective-permute-done | bytes 6176 | tf_op jit(solution)/shard_map/ppermute | solution.py:38
  126.0 5.6 %collective-permute-done.2.p2 = bf16[2,256,384]{2,1,0:T(8,128)(2,1)S(1)} collective-permute-done((bf16[2,256,384]{2,1,0:T(8,128)(2,1)S(1)}, bf16[2,256,384]{2,1,0:T(8,128)(2,1)S(1)}, u32[]{:S(2)}, u32[]{:S(2)}) %collective-permute-start.2) | collective-permute-done | bytes 393248 | tf_op jit(solution)/shard_map/ppermute | solution.py:38
  131.7 8.4 %collective-permute-done.3.p3 = bf16[2,256,384]{2,1,0:T(8,128)(2,1)} collective-permute-done((bf16[2,256,384]{2,1,0:T(8,128)(2,1)S(1)}, bf16[2,256,384]{2,1,0:T(8,128)(2,1)}, u32[]{:S(2)}, u32[]{:S(2)}) %collective-permute-start.3) | collective-permute-done | bytes 393248 | tf_op jit(solution)/shard_map/ppermute | solution.py:38
  162.1 6.5 %collective-permute-done.9.h1 = bf16[512,384]{1,0:T(8,128)(2,1)S(1)} collective-permute-done((bf16[512,384]{1,0:T(8,128)(2,1)S(1)}, bf16[512,384]{1,0:T(8,128)(2,1)S(1)}, u32[]{:S(2)}, u32[]{:S(2)}) %collective-permute-start.9) | collective-permute-done | bytes 393248 | tf_op jit(solution)/shard_map/ppermute | solution.py:38
  170.0 9.2 %collective-permute-done.10.h2 = bf16[512,384]{1,0:T(8,128)(2,1)S(1)} collective-permute-done((bf16[512,384]{1,0:T(8,128)(2,1)S(1)}, bf16[512,384]{1,0:T(8,128)(2,1)S(1)}, u32[]{:S(2)}, u32[]{:S(2)}) %collective-permute-start.10) | collective-permute-done | bytes 393248 | tf_op jit(solution)/shard_map/ppermute | solution.py:38
  186.9 5.4 %mix.1 = (f32[512,1536]{1,0:T(8,128)S(1)}, bf16[512,1536]{1,0:T(8,128)(2,1)S(1)}, f32[512,1]{1,0:T(8,128)S(1)}) custom-call(s32[8]{0:T(128)S(1)} %stack.133.spot, bf16[512,1536]{1,0:T(8,128)(2,1)S(1)} %copy-done.22, bf16[512,384]{1,0:T(8,128)(2,1)S(1)} %get-tuple-element.51.h0, bf16[512,384]{1,0:T(8,128)(2,1)S(1)} %collective-permute-done.9.h1, ...), custom_call_target="tpu_custom_call" | custom-call | flops 2415919104 | bytes 12582912 | tf_op jit(solution)/shard_map/mix/pallas_call | solution.py:260
  195.9 5.6 %collective-permute-done.16.g3 = bf16[2,256,384]{2,1,0:T(8,128)(2,1)} collective-permute-done((bf16[2,256,384]{2,1,0:T(8,128)(2,1)}, bf16[2,256,384]{2,1,0:T(8,128)(2,1)}, u32[]{:S(2)}, u32[]{:S(2)}) %collective-permute-start.16) | collective-permute-done | bytes 393248 | tf_op jit(solution)/shard_map/ppermute | solution.py:38
  201.4 15.5 %feed.1 = (bf16[512,1536]{1,0:T(8,128)(2,1)}, bf16[1024,512]{1,0:T(8,128)(2,1)S(1)}, bf16[1024,512]{1,0:T(8,128)(2,1)S(1)}, bf16[1024,512]{1,0:T(8,128)(2,1)}, b...) custom-call(s32[8]{0:T(128)S(1)} %stack.133.spot, ...), custom_call_target="tpu_custom_call" | custom-call | flops 8053063680 | bytes 20971520 | tf_op jit(solution)/shard_map/feed/pallas_call | solution.py:324
  225.8 7.9 %collective-permute-done.46.rest_0_ = bf16[16,3,64,768]{3,2,1,0:T(8,128)(2,1)S(1)} collective-permute-done((bf16[16,3,64,768]{3,2,1,0:T(8,128)(2,1)S(1)}, bf16[16,3,64,768]{3,2,1,0:T(8,128)(2,1)S(1)}, u32[]{:S(2)}, u32[]{:S(2)}) %collective-permute-start.46) | collective-permute-done | bytes 4718624 | tf_op jit(solution)/shard_map/ppermute | solution.py:38
  244.5 72.2 %all-to-all-done.4 = bf16[16,3,64,768]{3,2,1,0:T(8,128)(2,1)} async-done(((bf16[16,3,64,768]{3,2,1,0:T(8,128)(2,1)}), bf16[16,3,64,768]{3,2,1,0:T(8,128)(2,1)}, u32[]{:S(2)}, u32[]{:S(2)}) %all-to-all-start.4) | async-done | bytes 4718624 | tf_op jit(solution)/shard_map/all_to_all | solution.py:58
  333.4 7.6 %collective-permute-done.23.r1 = bf16[128,1536]{1,0:T(8,128)(2,1)S(1)} collective-permute-done((bf16[128,1536]{1,0:T(8,128)(2,1)}, bf16[128,1536]{1,0:T(8,128)(2,1)S(1)}, u32[]{:S(2)}, u32[]{:S(2)}) %collective-permute-start.23) | collective-permute-done | bytes 393248 | tf_op jit(solution)/shard_map/ppermute | solution.py:38
  341.0 5.6 %collective-permute-done.24.r2 = bf16[128,1536]{1,0:T(8,128)(2,1)S(1)} collective-permute-done((bf16[128,1536]{1,0:T(8,128)(2,1)}, bf16[128,1536]{1,0:T(8,128)(2,1)S(1)}, u32[]{:S(2)}, u32[]{:S(2)}) %collective-permute-start.24) | collective-permute-done | bytes 393248 | tf_op jit(solution)/shard_map/ppermute | solution.py:38
  363.7 5.8 %collective-permute-done.27.r2 = bf16[128,1536]{1,0:T(8,128)(2,1)S(1)} collective-permute-done((bf16[128,1536]{1,0:T(8,128)(2,1)S(1)}, bf16[128,1536]{1,0:T(8,128)(2,1)S(1)}, u32[]{:S(2)}, u32[]{:S(2)}) %collective-permute-start.27) | collective-permute-done | bytes 393248 | tf_op jit(solution)/shard_map/ppermute | solution.py:38
  372.1 8.6 %attend_backward.1 = (bf16[512,1536]{1,0:T(8,128)(2,1)}, bf16[384,512]{1,0:T(8,128)(2,1)S(1)}, f32[384,512]{1,0:T(8,128)S(1)}, bf16[384,512]{1,0:T(8,128)(2,1)S(1)}) custom-call(s32[8]{0:T(128)S(1)} %stack.133.spot, bf16[128,1536]{1,0:T(8,128)(2,1)S(1)} %get-tuple-element.65.r0, bf16[128,1536]{1,0:T(8,128)(2,1)S(1)} %collective-permute-done.26.r1, ...), custom_call_target="tpu_custom_call" | custom-call | flops 2113929216 | bytes 8388608 | tf_op jit(solution)/shard_map/attend_backward/pallas_call | solution.py:474
  406.4 12.9 %all-to-all-start.2 = ((bf16[16,72,768]{2,1,0:T(8,128)(2,1)}), bf16[16,72,768]{2,1,0:T(8,128)(2,1)}, u32[]{:S(2)}, u32[]{:S(2)}) async-start(bf16[16,72,768]{2,1,0:T(8,128)(2,1)} %bitcast.48), calls=%async_computation.2 | async-start | bytes 3538944 | tf_op jit(solution)/shard_map/all_to_all | solution.py:58
  429.8 15.5 %collective-permute-done.36 = f32[2,1536]{1,0:T(2,128)S(1)} collective-permute-done((f32[2,1536]{1,0:T(2,128)S(1)}, f32[2,1536]{1,0:T(2,128)S(1)}, u32[]{:S(2)}, u32[]{:S(2)}) %collective-permute-start.36) | collective-permute-done | bytes 12320 | tf_op jit(solution)/shard_map/ppermute | solution.py:38
  450.6 5.9 %collective-permute-start.40 = (f32[2,1536]{1,0:T(2,128)S(1)}, f32[2,1536]{1,0:T(2,128)}, u32[]{:S(2)}, u32[]{:S(2)}) collective-permute-start(f32[2,1536]{1,0:T(2,128)S(1)} %add.183), channel_id=1, source_target_pairs={{0,96},{32,64},{64,32},{96,0},{1,97},{33,65},{65,33},{97,1},{2,98}... | collective-permute-start | bytes 36872 | tf_op jit(solution)/shard_map/ppermute | solution.py:38
  465.5 8.6 %all-to-all-start.3 = ((bf16[16,2,72,384]{3,2,1,0:T(8,128)(2,1)}), bf16[16,2,72,384]{3,2,1,0:T(8,128)(2,1)S(1)}, u32[]{:S(2)}, u32[]{:S(2)}) async-start(bf16[16,2,72,384]{3,2,1,0:T(8,128)(2,1)} %broadcast_in_dim.44), calls=%async_computation.3 | async-start | bytes 3538944 | tf_op jit(solution)/shard_map/all_to_all | solution.py:64
  482.5 11.1 %collective-permute-done.41 = f32[2,1536]{1,0:T(2,128)S(1)} collective-permute-done((f32[2,1536]{1,0:T(2,128)S(1)}, f32[2,1536]{1,0:T(2,128)S(1)}, u32[]{:S(2)}, u32[]{:S(2)}) %collective-permute-start.41) | collective-permute-done | bytes 12320 | tf_op jit(solution)/shard_map/ppermute | solution.py:38
  502.6 7.4 %finish_units.1 = (f32[384,2048]{1,0:T(8,128)}, f32[384,2048]{1,0:T(8,128)}, f32[2048,384]{1,0:T(8,128)}) custom-call(bf16[16,2,3,64,384]{4,3,2,1,0:T(8,128)(2,1)S(1)} %bitcast.110), custom_call_target="tpu_custom_call" | custom-call | bytes 14680064 | tf_op jit(solution)/shard_map/finish_units/pallas_call | solution.py:601
  (347 shorter events, 182.7 us)
Async XLA Ops:
  7.2 83.6 %all-gather.5.cloned.1.call-start = ((), (), s32[]{:S(2)}) async-start(), calls=%async_computation.5 | async-start | bytes 5013504 | tf_op jit(solution)/shard_map/all_gather | solution.py:54
  29.3 78.6 %all-to-all-start.1 = ((bf16[16,2,48,768]{3,2,1,0:T(8,128)(2,1)}), bf16[16,2,48,768]{3,2,1,0:T(8,128)(2,1)}, u32[]{:S(2)}, u32[]{:S(2)}) async-start(bf16[16,2,48,768]{3,2,1,0:T(8,128)(2,1)} %broadcast_in_dim.20), calls=%async_computation.1 | async-start | bytes 4718592 | tf_op jit(solution)/shard_map/all_to_all | solution.py:64
  90.8 110.6 %collective-permute-start.18 = (bf16[16,3,64,768]{3,2,1,0:T(8,128)(2,1)}, bf16[16,3,64,768]{3,2,1,0:T(8,128)(2,1)}, u32[]{:S(2)}, u32[]{:S(2)}) collective-permute-start(bf16[16,3,64,768]{3,2,1,0:T(8,128)(2,1)} %bitcast.107), channel_id=1, source_target_pairs={{0,2},{2,0},{1,3},{3,1},{4,6},{6,4},{5,7},{7,5},{8,10},{10,8},{9,1... | collective-permute-start | bytes 14155784 | tf_op jit(solution)/shard_map/ppermute | solution.py:38
  107.8 32.3 %collective-permute-start.7 = (bf16[768,768]{1,0:T(8,128)(2,1)S(1)}, bf16[768,768]{1,0:T(8,128)(2,1)S(1)}, u32[]{:S(2)}, u32[]{:S(2)}) collective-permute-start(bf16[768,768]{1,0:T(8,128)(2,1)S(1)} %pad_maximum_fusion.own), channel_id=1, source_target_pairs={{0,2},{2,0},{1,3},{3,1},{4,6},{6,4},{5,7},{7,5},{8,10},{10,8},{9,1... | collective-permute-start | bytes 3538952 | tf_op jit(solution)/shard_map/ppermute | solution.py:38
  107.9 75.6 %collective-permute-start.12 = (bf16[16,2,48,768]{3,2,1,0:T(8,128)(2,1)}, bf16[16,2,48,768]{3,2,1,0:T(8,128)(2,1)}, u32[]{:S(2)}, u32[]{:S(2)}) collective-permute-start(bf16[16,2,48,768]{3,2,1,0:T(8,128)(2,1)} %all-to-all-done.1.own.wown), channel_id=1, source_target_pairs={{0,2},{2,0},{1,3},{3,1},{4,6},{6,4},{5,7},{7,5},{8,10},{10,8},{9,1... | collective-permute-start | bytes 7077896 | tf_op jit(solution)/shard_map/ppermute | solution.py:38
  158.1 21.1 %collective-permute-start.10 = (bf16[512,384]{1,0:T(8,128)(2,1)S(1)}, bf16[512,384]{1,0:T(8,128)(2,1)S(1)}, u32[]{:S(2)}, u32[]{:S(2)}) collective-permute-start(bf16[512,384]{1,0:T(8,128)(2,1)S(1)} %get-tuple-element.51.h0), channel_id=1, source_target_pairs={{0,1},{1,0},{4,5},{5,4},{2,3},{3,2},{6,7},{7,6},{8,9},{9,8},{12,13... | collective-permute-start | bytes 1179656 | tf_op jit(solution)/shard_map/ppermute | solution.py:38
  160.8 20.2 %collective-permute-start.11 = (bf16[512,384]{1,0:T(8,128)(2,1)S(1)}, bf16[512,384]{1,0:T(8,128)(2,1)S(1)}, u32[]{:S(2)}, u32[]{:S(2)}) collective-permute-start(bf16[512,384]{1,0:T(8,128)(2,1)S(1)} %get-tuple-element.51.h0), channel_id=1, source_target_pairs={{0,5},{1,4},{4,1},{5,0},{2,7},{3,6},{6,3},{7,2},{8,13},{9,12},{12,... | collective-permute-start | bytes 1179656 | tf_op jit(solution)/shard_map/ppermute | solution.py:38
  168.6 27.3 %collective-permute-start.14 = (bf16[2,256,384]{2,1,0:T(8,128)(2,1)}, bf16[2,256,384]{2,1,0:T(8,128)(2,1)S(1)}, u32[]{:S(2)}, u32[]{:S(2)}) collective-permute-start(bf16[2,256,384]{2,1,0:T(8,128)(2,1)} %pad_maximum_fusion.2.g0), channel_id=1, source_target_pairs={{0,4},{1,5},{4,0},{5,1},{2,6},{3,7},{6,2},{7,3},{8,12},{9,13},{12,... | collective-permute-start | bytes 1179656 | tf_op jit(solution)/shard_map/ppermute | solution.py:38
  181.8 19.6 %collective-permute-start.16 = (bf16[2,256,384]{2,1,0:T(8,128)(2,1)}, bf16[2,256,384]{2,1,0:T(8,128)(2,1)}, u32[]{:S(2)}, u32[]{:S(2)}) collective-permute-start(bf16[2,256,384]{2,1,0:T(8,128)(2,1)} %pad_maximum_fusion.2.g0), channel_id=1, source_target_pairs={{0,5},{1,4},{4,1},{5,0},{2,7},{3,6},{6,3},{7,2},{8,13},{9,12},{12,... | collective-permute-start | bytes 1179656 | tf_op jit(solution)/shard_map/ppermute | solution.py:38
  239.1 77.5 %all-to-all-start.4 = ((bf16[16,3,64,768]{3,2,1,0:T(8,128)(2,1)}), bf16[16,3,64,768]{3,2,1,0:T(8,128)(2,1)}, u32[]{:S(2)}, u32[]{:S(2)}) async-start(bf16[16,3,64,768]{3,2,1,0:T(8,128)(2,1)} %copy-done.2), calls=%async_computation.4 | async-start | bytes 9437184 | tf_op jit(solution)/shard_map/all_to_all | solution.py:58
  244.5 255.7 %all-gather.7.cloned.1.call-start = ((), (), s32[]{:S(2)}) async-start(), calls=%async_computation.6 | async-start | bytes 5013504 | tf_op jit(solution)/shard_map/all_gather | solution.py:54
  328.7 17.8 %collective-permute-start.24 = (bf16[128,1536]{1,0:T(8,128)(2,1)}, bf16[128,1536]{1,0:T(8,128)(2,1)S(1)}, u32[]{:S(2)}, u32[]{:S(2)}) collective-permute-start(bf16[128,1536]{1,0:T(8,128)(2,1)} %copy-done.60), channel_id=1, source_target_pairs={{0,1},{1,0},{4,5},{5,4},{2,3},{3,2},{6,7},{7,6},{8,9},{9,8},{12,13... | collective-permute-start | bytes 1179656 | tf_op jit(solution)/shard_map/ppermute | solution.py:38
  397.7 22.7 %collective-permute-start.21 = (bf16[2,256,384]{2,1,0:T(8,128)(2,1)S(1)}, bf16[2,256,384]{2,1,0:T(8,128)(2,1)S(1)}, u32[]{:S(2)}, u32[]{:S(2)}) collective-permute-start(bf16[2,256,384]{2,1,0:T(8,128)(2,1)S(1)} %get-tuple-element.58), channel_id=1, source_target_pairs={{0,5},{1,4},{4,1},{5,0},{2,7},{3,6},{6,3},{7,2},{8,13},{9,12},{12,... | collective-permute-start | bytes 1179656 | tf_op jit(solution)/shard_map/ppermute | solution.py:38
  399.0 21.5 %collective-permute-start.20 = (bf16[2,256,384]{2,1,0:T(8,128)(2,1)S(1)}, bf16[2,256,384]{2,1,0:T(8,128)(2,1)S(1)}, u32[]{:S(2)}, u32[]{:S(2)}) collective-permute-start(bf16[2,256,384]{2,1,0:T(8,128)(2,1)S(1)} %get-tuple-element.57), channel_id=1, source_target_pairs={{0,1},{1,0},{4,5},{5,4},{2,3},{3,2},{6,7},{7,6},{8,9},{9,8},{12,13... | collective-permute-start | bytes 1179656 | tf_op jit(solution)/shard_map/ppermute | solution.py:38
  399.0 21.5 %collective-permute-start.19 = (bf16[2,256,384]{2,1,0:T(8,128)(2,1)S(1)}, bf16[2,256,384]{2,1,0:T(8,128)(2,1)}, u32[]{:S(2)}, u32[]{:S(2)}) collective-permute-start(bf16[2,256,384]{2,1,0:T(8,128)(2,1)S(1)} %get-tuple-element.56), channel_id=1, source_target_pairs={{0,4},{1,5},{4,0},{5,1},{2,6},{3,7},{6,2},{7,3},{8,12},{9,13},{12,... | collective-permute-start | bytes 1179656 | tf_op jit(solution)/shard_map/ppermute | solution.py:38
  406.4 51.6 %all-to-all-start.2 = ((bf16[16,72,768]{2,1,0:T(8,128)(2,1)}), bf16[16,72,768]{2,1,0:T(8,128)(2,1)}, u32[]{:S(2)}, u32[]{:S(2)}) async-start(bf16[16,72,768]{2,1,0:T(8,128)(2,1)} %bitcast.48), calls=%async_computation.2 | async-start | bytes 3538944 | tf_op jit(solution)/shard_map/all_to_all | solution.py:58
  423.1 33.4 %collective-permute-start.32 = (bf16[2,256,384]{2,1,0:T(8,128)(2,1)S(1)}, bf16[2,256,384]{2,1,0:T(8,128)(2,1)S(1)}, u32[]{:S(2)}, u32[]{:S(2)}) collective-permute-start(bf16[2,256,384]{2,1,0:T(8,128)(2,1)S(1)} %copy-done.56), channel_id=1, source_target_pairs={{0,5},{1,4},{4,1},{5,0},{2,7},{3,6},{6,3},{7,2},{8,13},{9,12},{12,... | collective-permute-start | bytes 1179656 | tf_op jit(solution)/shard_map/ppermute | solution.py:38
  424.7 32.8 %collective-permute-start.31 = (bf16[2,256,384]{2,1,0:T(8,128)(2,1)S(1)}, bf16[2,256,384]{2,1,0:T(8,128)(2,1)S(1)}, u32[]{:S(2)}, u32[]{:S(2)}) collective-permute-start(bf16[2,256,384]{2,1,0:T(8,128)(2,1)S(1)} %copy-done.54), channel_id=1, source_target_pairs={{0,1},{1,0},{4,5},{5,4},{2,3},{3,2},{6,7},{7,6},{8,9},{9,8},{12,13... | collective-permute-start | bytes 1179656 | tf_op jit(solution)/shard_map/ppermute | solution.py:38
  425.5 32.0 %collective-permute-start.30 = (bf16[2,256,384]{2,1,0:T(8,128)(2,1)S(1)}, bf16[2,256,384]{2,1,0:T(8,128)(2,1)S(1)}, u32[]{:S(2)}, u32[]{:S(2)}) collective-permute-start(bf16[2,256,384]{2,1,0:T(8,128)(2,1)S(1)} %copy-done.52), channel_id=1, source_target_pairs={{0,4},{1,5},{4,0},{5,1},{2,6},{3,7},{6,2},{7,3},{8,12},{9,13},{12,... | collective-permute-start | bytes 1179656 | tf_op jit(solution)/shard_map/ppermute | solution.py:38
  450.6 25.5 %collective-permute-start.40 = (f32[2,1536]{1,0:T(2,128)S(1)}, f32[2,1536]{1,0:T(2,128)}, u32[]{:S(2)}, u32[]{:S(2)}) collective-permute-start(f32[2,1536]{1,0:T(2,128)S(1)} %add.183), channel_id=1, source_target_pairs={{0,96},{32,64},{64,32},{96,0},{1,97},{33,65},{65,33},{97,1},{2,98}... | collective-permute-start | bytes 36872 | tf_op jit(solution)/shard_map/ppermute | solution.py:38
  456.5 19.6 %collective-permute-start.39 = (f32[2,1536]{1,0:T(2,128)S(1)}, f32[2,1536]{1,0:T(2,128)}, u32[]{:S(2)}, u32[]{:S(2)}) collective-permute-start(f32[2,1536]{1,0:T(2,128)S(1)} %add.183), channel_id=1, source_target_pairs={{0,64},{32,96},{64,0},{96,32},{1,65},{33,97},{65,1},{97,33},{2,66}... | collective-permute-start | bytes 36872 | tf_op jit(solution)/shard_map/ppermute | solution.py:38
  456.5 19.6 %collective-permute-start.38 = (f32[2,1536]{1,0:T(2,128)S(1)}, f32[2,1536]{1,0:T(2,128)}, u32[]{:S(2)}, u32[]{:S(2)}) collective-permute-start(f32[2,1536]{1,0:T(2,128)S(1)} %add.183), channel_id=1, source_target_pairs={{0,32},{32,0},{64,96},{96,64},{1,33},{33,1},{65,97},{97,65},{2,34}... | collective-permute-start | bytes 36872 | tf_op jit(solution)/shard_map/ppermute | solution.py:38
  465.5 30.4 %all-to-all-start.3 = ((bf16[16,2,72,384]{3,2,1,0:T(8,128)(2,1)}), bf16[16,2,72,384]{3,2,1,0:T(8,128)(2,1)S(1)}, u32[]{:S(2)}, u32[]{:S(2)}) async-start(bf16[16,2,72,384]{3,2,1,0:T(8,128)(2,1)} %broadcast_in_dim.44), calls=%async_computation.3 | async-start | bytes 3538944 | tf_op jit(solution)/shard_map/all_to_all | solution.py:64
  476.0 18.2 %collective-permute-start.34 = (f32[256,384]{1,0:T(8,128)S(1)}, f32[256,384]{1,0:T(8,128)S(1)}, u32[]{:S(2)}, u32[]{:S(2)}) collective-permute-start(f32[256,384]{1,0:T(8,128)S(1)} %slice_bitcast_fusion), channel_id=1, source_target_pairs={{0,2},{2,0},{1,3},{3,1},{4,6},{6,4},{5,7},{7,5},{8,10},{10,8},{9,1... | collective-permute-start | bytes 1179656 | tf_op jit(solution)/shard_map/ppermute | solution.py:38
  (115 other events, 1396.8 us)
Sparse Core Ops, SparseCore 0:
  16.4 74.3 all-gather.4
  328.8 58.8 all-gather.6
